TPU v7x, 32 devices: a whole 2x2x4 slice. The times are simulated.
32 devices in a mesh: row: 8 (over z, y), col: 4 (over x, core).
Axes of the slice: x: 2, y: 2, z: 4, core: 2. Of those that a mesh axis runs over, the one named last changes fastest.
Arguments:
- object_field: float32 [2, 3, 2048, 1024], P(None, None, 'row', 'col'), may hold values from -1 to 1
- probe: float32 [2, 128, 128], replicated, may hold values from -4 to 4
- propagator: float32 [128, 128], replicated, may hold values from -3.140625 to 3.140625
- measured: float32 [8, 4, 6, 128, 128], P('row', 'col'), may hold values from 0 to 1
- offsets: int32 [8, 4, 6, 2], P('row', 'col'), may hold values from 0 to 255
Outputs:
- updated: float32 [2, 3, 2048, 1024], P(None, None, 'row', 'col')
Inputs may be any that keep to these rules, and one draw needn't show every extreme that they name: `offsets`: entry 0 is the row offset and entry 1 the column offset of a window inside its tile.
All inputs are finite; a program needn't handle non-finite values.
Results may differ from a plain program's by a relative error of at most 0.0003.
Values sent between devices are 32-bit elements; how exact they have to be, the bound alone decides.
A program may use at most 64 MiB of HBM per device.

v0:
```python
import jax
import jax.numpy as jnp
import numpy as np
from jax import lax
from jax.experimental import pallas as pl
from jax.experimental.pallas import tpu as pltpu
from jax.sharding import PartitionSpec as P

ITERS = 2
STEP = 0.05
SUB = 8
F32, BF16 = jnp.float32, jnp.bfloat16


def passed_along(block, axis, distance):
    n = lax.axis_size(axis)
    return lax.ppermute(block, axis, [((i - distance) % n, i) for i in range(n)])


def tables(h):
    k = np.arange(h)
    angle = (k[:, None] * k[None, :] % h) * (-2.0 * np.pi / h)
    c, s = np.cos(angle) / np.sqrt(h), np.sin(angle) / np.sqrt(h)

    def halves(m):
        m = m.astype(np.float32)
        high = m.astype(jnp.bfloat16)
        return high, (m - high.astype(np.float32)).astype(jnp.bfloat16)

    ah, al = halves(np.block([[c, s], [-s, c]]))
    bh, bl = halves(np.block([[c, -s], [s, c]]))
    right = [np.concatenate([x, x, y], 0) for x, y in ((ah, al), (bh, bl))]
    left = [np.concatenate([x, x, y], 1) for x, y in ((bh, bl), (ah, al))]
    return np.stack(right), np.stack(left)


def split(x):
    high = x.astype(BF16)
    return high, (x - high.astype(F32)).astype(BF16)


def mul_right(x, table):
    high, low = split(x)
    return jnp.dot(jnp.concatenate([high, low, high], 1), table, preferred_element_type=F32)


def mul_left(x, table):
    high, low = split(x)
    return jnp.dot(table, jnp.concatenate([high, low, high], 0), preferred_element_type=F32)


def to_left(x, h, n):
    return jnp.concatenate(
        [jnp.concatenate([x[p * h:(p + 1) * h, k * h:(k + 1) * h] for p in range(n)], 1) for k in range(2)], 0)


def to_right(x, h, n):
    return jnp.concatenate(
        [jnp.concatenate([x[k * h:(k + 1) * h, p * h:(p + 1) * h] for k in range(2)], 1) for p in range(n)], 0)


def dft(x, tab, h, n):
    return mul_left(to_left(mul_right(x, tab[0][0]), h, n), tab[1][0])


def idft(x, tab, h, n):
    return mul_right(to_right(mul_left(x, tab[1][1]), h, n), tab[0][1])


def propagate(x, tab, phase, sign, h, n):
    y = dft(x, tab, h, n)
    cr, ci = phase[0], phase[1] * sign
    cr, ci = (jnp.concatenate([v] * n, 1) for v in (cr, ci))
    a, b = y[:h], y[h:]
    return idft(jnp.concatenate([a * cr - b * ci, a * ci + b * cr], 0), tab, h, n)


def times(x, o, sign, h):
    a, b, c, d = x[:, :h], x[:, h:], o[:, :h], o[:, h:]
    if sign < 0:
        return jnp.concatenate([a * c + b * d, b * c - a * d], 1)
    return jnp.concatenate([a * c - b * d, a * d + b * c], 1)


def gather(ext, r, c, h):
    lane = lax.broadcasted_iota(jnp.int32, (h + SUB, h), 1)
    sub = lax.broadcasted_iota(jnp.int32, (h // SUB, SUB, h), 1)
    q, m, t = c // h, c % h, r % SUB
    parts = []
    for k in range(2):
        lines = ext[k, pl.ds(pl.multiple_of(r - t, SUB), h + SUB), pl.ds(pl.multiple_of(q * h, h), 2 * h)]
        mixed = jnp.where(lane >= m, lines[:, :h], lines[:, h:])
        mixed = pltpu.roll(mixed, (h - m) % h, 1).reshape(h // SUB + 1, SUB, h)
        mixed = jnp.where(sub >= t, mixed[:-1], mixed[1:])
        parts.append(pltpu.roll(mixed, (SUB - t) % SUB, 1).reshape(h, h))
    return jnp.concatenate(parts, 1)


def scatter(acc, g, r, c, h):
    lane = lax.broadcasted_iota(jnp.int32, (h + SUB, h), 1)
    sub = lax.broadcasted_iota(jnp.int32, (h // SUB + 1, SUB, h), 1)
    q, m, t = c // h, c % h, r % SUB
    empty = jnp.zeros((1, SUB, h), F32)
    for k in range(2):
        rolled = pltpu.roll(g[:, k * h:(k + 1) * h].reshape(h // SUB, SUB, h), t, 1)
        rolled = jnp.where(sub >= t, jnp.concatenate([rolled, empty], 0), jnp.concatenate([empty, rolled], 0))
        rolled = pltpu.roll(rolled.reshape(h + SUB, h), m, 1)
        keep = lane >= m
        pair = jnp.concatenate([jnp.where(keep, rolled, 0.0), jnp.where(keep, 0.0, rolled)], 1)
        at = (k, pl.ds(pl.multiple_of(r - t, SUB), h + SUB), pl.ds(pl.multiple_of(q * h, h), 2 * h))
        acc[at] = acc[at] + pair


def groups(n):
    size = 2 if n % 2 == 0 else 1
    return [list(range(i, i + size)) for i in range(0, n, size)]


def fill(ext, tall, right):
    w = tall.shape[2]
    ext[:, :, :w] = tall[...]
    ext[:, :, w:] = right[...]


def read_windows(ext, offs, ps, h):
    return jnp.concatenate([gather(ext, offs[p, 0], offs[p, 1], h) for p in ps], 0)


def tiled_probe(probe, n):
    one = jnp.concatenate([probe[0], probe[1]], 1)
    return jnp.concatenate([one] * n, 0)


def tab_of(tr, tl):
    return ([tr[0], tr[1]], [tl[0], tl[1]])


def rows_of(ps, h):
    return slice(ps[0] * h, (ps[-1] + 1) * h)


def k_first(offs, tall, right, probe, phase, tr, tl, w_out, ext):
    h, tab = probe.shape[1], tab_of(tr, tl)
    fill(ext, tall, right)
    for ps in groups(offs.shape[0]):
        n = len(ps)
        x = times(tiled_probe(probe, n), read_windows(ext, offs, ps, h), 1, h)
        w_out[rows_of(ps, h)] = propagate(x, tab, phase, 1.0, h, n)


def k_second(offs, tall, right, w_in, phase, tr, tl, w_out, o_out, ext):
    h, tab = phase.shape[1], tab_of(tr, tl)
    fill(ext, tall, right)
    for ps in groups(offs.shape[0]):
        n, rows = len(ps), rows_of(ps, h)
        o = read_windows(ext, offs, ps, h)
        o_out[rows] = o
        w_out[rows] = propagate(times(w_in[rows], o, 1, h), tab, phase, 1.0, h, n)


def emit(acc, gl, gr):
    w = gl.shape[2]
    gl[...] = acc[:, :, :w]
    gr[...] = acc[:, :, w:]


def k_last(offs, tall, right, w_in, measured, tr, tl, gl, gr, g_out, ext, acc):
    h, tab = measured.shape[1], tab_of(tr, tl)
    fill(ext, tall, right)
    acc[...] = jnp.zeros_like(acc)
    for ps in groups(offs.shape[0]):
        n, rows = len(ps), rows_of(ps, h)
        o = read_windows(ext, offs, ps, h)
        w = w_in[rows]
        far = dft(times(w, o, 1, h), tab, h, n)
        a, b = far[:h], far[h:]
        target = jnp.concatenate([measured[p] for p in ps], 1)
        f = 4.0 * (a * a + b * b - target)
        g = idft(jnp.concatenate([a * f, b * f], 0), tab, h, n)
        go = times(g, w, -1, h)
        g_out[rows] = times(g, o, -1, h)
        for i, p in enumerate(ps):
            scatter(acc, go[i * h:(i + 1) * h], offs[p, 0], offs[p, 1], h)
    emit(acc, gl, gr)


def k_back(offs, g_in, w_in, o_in, phase, tr, tl, gl, gr, g_out, acc):
    h, tab = phase.shape[1], tab_of(tr, tl)
    acc[...] = jnp.zeros_like(acc)
    for ps in groups(offs.shape[0]):
        n, rows = len(ps), rows_of(ps, h)
        g = propagate(g_in[rows], tab, phase, -1.0, h, n)
        go = times(g, w_in[rows], -1, h)
        g_out[rows] = times(g, o_in[rows], -1, h)
        for i, p in enumerate(ps):
            scatter(acc, go[i * h:(i + 1) * h], offs[p, 0], offs[p, 1], h)
    emit(acc, gl, gr)


def k_back_first(offs, g_in, probe, phase, tr, tl, gl, gr, acc):
    h, tab = phase.shape[1], tab_of(tr, tl)
    acc[...] = jnp.zeros_like(acc)
    for ps in groups(offs.shape[0]):
        n, rows = len(ps), rows_of(ps, h)
        g = propagate(g_in[rows], tab, phase, -1.0, h, n)
        go = times(g, tiled_probe(probe, n), -1, h)
        for i, p in enumerate(ps):
            scatter(acc, go[i * h:(i + 1) * h], offs[p, 0], offs[p, 1], h)
    emit(acc, gl, gr)


def on_device(object_field, probe, propagator, measured, offsets):
    slices, tile_r, tile_c = object_field.shape[1:]
    h, pos = probe.shape[1], offsets.shape[2]
    offs = offsets.reshape(pos, 2)
    target = measured.reshape(pos, h, h)
    phase = jnp.stack([jnp.cos(propagator), jnp.sin(propagator)])
    tr, tl = (jnp.asarray(t) for t in tables(h))

    wave = jax.ShapeDtypeStruct((pos * h, 2 * h), F32)
    ext = pltpu.VMEM((2, tile_r + h, tile_c + h), F32)
    grad = [jax.ShapeDtypeStruct((2, tile_r + h, tile_c), F32), jax.ShapeDtypeStruct((2, tile_r + h, h), F32)]
    flops = 2 * 2 * 2 * 3 * pos * h * (2 * h) ** 2
    cost = pl.CostEstimate(flops=flops, bytes_accessed=6_000_000, transcendentals=0)

    def call(body, outs, scratch, *args):
        vmem = pl.BlockSpec(memory_space=pltpu.VMEM)
        return pl.pallas_call(
            body,
            out_shape=outs,
            in_specs=[pl.BlockSpec(memory_space=pltpu.SMEM)] + [vmem] * len(args),
            out_specs=[vmem] * len(outs),
            scratch_shapes=scratch,
            cost_estimate=cost,
            compiler_params=pltpu.CompilerParams(vmem_limit_bytes=40 * 1024 * 1024),
        )(offs, *args)

    tall, right = [], []
    for s in range(slices):
        own = object_field[:, s]
        tall.append(jnp.concatenate([own, passed_along(own[:, :h], "row", -1)], 1))
    for s in range(slices):
        right.append(passed_along(tall[s][:, :, :h], "col", -1))

    result = [None] * slices
    for step in range(ITERS):
        waves, objects = [None], [None]
        (w,) = call(k_first, [wave], [ext], tall[0], right[0], probe, phase, tr, tl)
        waves.append(w)
        for s in range(1, slices - 1):
            w, o = call(k_second, [wave, wave], [ext], tall[s], right[s], waves[s], phase, tr, tl)
            waves.append(w)
            objects.append(o)
        s = slices - 1
        grads = [None] * slices
        *grads[s], g = call(k_last, grad + [wave], [ext, ext], tall[s], right[s], waves[s], target, tr, tl)
        for s in range(slices - 2, 0, -1):
            *grads[s], g = call(k_back, grad + [wave], [ext], g, waves[s], objects[s], phase, tr, tl)
        grads[0] = call(k_back_first, grad, [ext], g, probe, phase, tr, tl)
        last = step + 1 == ITERS
        for s in range(slices - 1, -1, -1):
            gl, gr = grads[s]
            total = gl.at[:, :, :h].add(passed_along(gr, "col", 1))
            above = passed_along(total[:, tile_r:], "row", 1)
            if last:
                result[s] = tall[s][:, :tile_r] - STEP * total[:, :tile_r].at[:, :h].add(above)
            else:
                below = passed_along(total[:, :h], "row", -1)
                total = total.at[:, :h].add(above).at[:, tile_r:].add(below)
                tall[s] = tall[s] - STEP * total
                right[s] = passed_along(tall[s][:, :, :h], "col", -1)
    return jnp.stack(result, 1)


def solution(mesh):
    return jax.shard_map(
        on_device,
        mesh=mesh,
        in_specs=(
            P(None, None, "row", "col"),
            P(),
            P(),
            P("row", "col", None, None, None),
            P("row", "col", None, None),
        ),
        out_specs=P(None, None, "row", "col"),
        check_vma=False,
    )
```

profile of v0, /device:TPU:0, one launch (start us, length us, event | category | flops | bytes accessed | tf_op | source)
XLA Modules:
  0.0 142.9 jit_solution(2398998479682268131)
XLA Ops:
  1.5 6.1 %collective-permute-start.3 = (f32[2,128,256]{2,1,0:T(8,128)S(1)}, f32[2,128,256]{2,1,0:T(8,128)S(1)}, u32[]{:S(2)}, u32[]{:S(2)}) collective-permute-start(f32[2,128,256]{2,1,0:T(8,128)S(1)} %slice.481), channel_id=1, source_target_pairs={{4,0},{8,4},{12,8},{16,12},{20,16},{24,20},{28,24},{0,28},{5,1},{9... | collective-permute-start | bytes 786440 | tf_op jit(solution)/shard_map/ppermute | solution.py:17
  10.0 4.3 %collective-permute-done.3 = f32[2,128,256]{2,1,0:T(8,128)S(1)} collective-permute-done((f32[2,128,256]{2,1,0:T(8,128)S(1)}, f32[2,128,256]{2,1,0:T(8,128)S(1)}, u32[]{:S(2)}, u32[]{:S(2)}) %collective-permute-start.3) | collective-permute-done | bytes 262176 | tf_op jit(solution)/shard_map/ppermute | solution.py:17
  14.4 5.5 %collective-permute-done.1 = f32[2,128,256]{2,1,0:T(8,128)S(1)} collective-permute-done((f32[2,128,256]{2,1,0:T(8,128)S(1)}, f32[2,128,256]{2,1,0:T(8,128)S(1)}, u32[]{:S(2)}, u32[]{:S(2)}) %collective-permute-start.1) | collective-permute-done | bytes 262176 | tf_op jit(solution)/shard_map/ppermute | solution.py:17
  20.0 4.4 %collective-permute-done = f32[2,128,256]{2,1,0:T(8,128)S(1)} collective-permute-done((f32[2,128,256]{2,1,0:T(8,128)S(1)}, f32[2,128,256]{2,1,0:T(8,128)S(1)}, u32[]{:S(2)}, u32[]{:S(2)}) %collective-permute-start) | collective-permute-done | bytes 262176 | tf_op jit(solution)/shard_map/ppermute | solution.py:17
  24.7 5.1 %collective-permute-done.5.right = f32[2,384,128]{2,1,0:T(8,128)S(1)} collective-permute-done((f32[2,384,128]{2,1,0:T(8,128)S(1)}, f32[2,384,128]{2,1,0:T(8,128)S(1)}, u32[]{:S(2)}, u32[]{:S(2)}) %collective-permute-start.5) | collective-permute-done | bytes 393248 | tf_op jit(solution)/shard_map/ppermute | solution.py:17
  29.8 3.8 %shard_map.73.w_in = f32[768,256]{1,0:T(8,128)S(1)} custom-call(s32[6,2]{1,0:T(8,128)S(1)} %copy.15.offs, f32[2,384,256]{2,1,0:T(8,128)S(1)} %pad_maximum_fusion.1.tall, f32[2,384,128]{2,1,0:T(8,128)S(1)} %collective-permute-done.5.right, f32[2,128,128]{2,1,0:T(8,128)S(1)} %copy-done.1, f32[2,128,128]{2,1,0:T(8,128)S(1)} %pad_maximum_fusion.4.phase, ...), custom_call_target="tpu_custom_call" | custom-call | flops 1207959552 | bytes 6000000 | tf_op jit(solution)/shard_map/pallas_call | solution.py:228
  33.7 3.8 %shard_map.74 = (f32[768,256]{1,0:T(8,128)S(1)}, f32[768,256]{1,0:T(8,128)S(1)}) custom-call(s32[6,2]{1,0:T(8,128)S(1)} %copy.15.offs, f32[2,384,256]{2,1,0:T(8,128)S(1)} %pad_maximum_fusion.3.tall, f32[2,384,128]{2,1,0:T(8,128)S(1)} %collective-permute-done.4.right, f32[768,256]{1,0:T(8,128)S(1)} %shard_map.73.w_in, ...), custom_call_target="tpu_custom_call" | custom-call | flops 1207959552 | bytes 6000000 | tf_op jit(solution)/shard_map/pallas_call | solution.py:228
  37.5 4.1 %shard_map.75 = (f32[2,384,256]{2,1,0:T(8,128)S(1)}, f32[2,384,128]{2,1,0:T(8,128)S(1)}, f32[768,256]{1,0:T(8,128)S(1)}) custom-call(s32[6,2]{1,0:T(8,128)S(1)} %copy.15.offs, f32[2,384,256]{2,1,0:T(8,128)S(1)} %pad_maximum_fusion.2.tall, f32[2,384,128]{2,1,0:T(8,128)S(1)} %collective-permute-done.2.right, f32[768,256]{1,0:T(8,128)S(1)} %get-tuple-element.205.w_in, ...), custom_call_target="tpu_custom_call" | custom-call | flops 1207959552 | bytes 6000000 | tf_op jit(solution)/shard_map/pallas_call | solution.py:228
  41.7 4.0 %shard_map.76 = (f32[2,384,256]{2,1,0:T(8,128)S(1)}, f32[2,384,128]{2,1,0:T(8,128)S(1)}, f32[768,256]{1,0:T(8,128)S(1)}) custom-call(s32[6,2]{1,0:T(8,128)S(1)} %copy.15.offs, f32[768,256]{1,0:T(8,128)S(1)} %get-tuple-element.206.g_in, f32[768,256]{1,0:T(8,128)S(1)} %shard_map.73.w_in, f32[768,256]{1,0:T(8,128)S(1)} %get-tuple-element.207.o_in, ...), custom_call_target="tpu_custom_call" | custom-call | flops 1207959552 | bytes 6000000 | tf_op jit(solution)/shard_map/pallas_call | solution.py:228
  45.7 4.0 %shard_map.77 = (f32[2,384,256]{2,1,0:T(8,128)S(1)}, f32[2,384,128]{2,1,0:T(8,128)S(1)}) custom-call(s32[6,2]{1,0:T(8,128)S(1)} %copy.15.offs, f32[768,256]{1,0:T(8,128)S(1)} %get-tuple-element.208.g_in, f32[2,128,128]{2,1,0:T(8,128)S(1)} %copy-done.1, f32[2,128,128]{2,1,0:T(8,128)S(1)} %pad_maximum_fusion.4.phase, bf16[2,768,256]{2,1,0:T(8,128)(2,1)S(1)} %copy-done.3, ...), custom_call_target="tpu_custom_call" | custom-call | flops 1207959552 | bytes 6000000 | tf_op jit(solution)/shard_map/pallas_call | solution.py:228
  52.1 5.0 %collective-permute-done.6 = f32[2,384,128]{2,1,0:T(8,128)S(1)} collective-permute-done((f32[2,384,128]{2,1,0:T(8,128)S(1)}, f32[2,384,128]{2,1,0:T(8,128)S(1)}, u32[]{:S(2)}, u32[]{:S(2)}) %collective-permute-start.6) | collective-permute-done | bytes 393248 | tf_op jit(solution)/shard_map/ppermute | solution.py:17
  57.5 3.7 %collective-permute-done.13 = f32[2,384,128]{2,1,0:T(8,128)S(1)} collective-permute-done((f32[2,384,128]{2,1,0:T(8,128)S(1)}, f32[2,384,128]{2,1,0:T(8,128)S(1)}, u32[]{:S(2)}, u32[]{:S(2)}) %collective-permute-start.13) | collective-permute-done | bytes 393248 | tf_op jit(solution)/shard_map/ppermute | solution.py:17
  71.2 6.6 %collective-permute-done.14 = f32[2,128,256]{2,1,0:T(8,128)S(1)} collective-permute-done((f32[2,128,256]{2,1,0:T(8,128)S(1)}, f32[2,128,256]{2,1,0:T(8,128)S(1)}, u32[]{:S(2)}, u32[]{:S(2)}) %collective-permute-start.14) | collective-permute-done | bytes 262176 | tf_op jit(solution)/shard_map/ppermute | solution.py:17
  77.8 7.3 %collective-permute-start.15 = (f32[2,128,256]{2,1,0:T(8,128)S(1)}, f32[2,128,256]{2,1,0:T(8,128)S(1)}, u32[]{:S(2)}, u32[]{:S(2)}) collective-permute-start(f32[2,128,256]{2,1,0:T(8,128)S(1)} %get-tuple-element.230), channel_id=1, source_target_pairs={{4,0},{8,4},{12,8},{16,12},{20,16},{24,20},{28,24},{0,28},{5,1},{9... | collective-permute-start | bytes 786440 | tf_op jit(solution)/shard_map/ppermute | solution.py:17
  85.2 4.2 %collective-permute-start.11 = (f32[2,128,256]{2,1,0:T(8,128)S(1)}, f32[2,128,256]{2,1,0:T(8,128)S(1)}, u32[]{:S(2)}, u32[]{:S(2)}) collective-permute-start(f32[2,128,256]{2,1,0:T(8,128)S(1)} %get-tuple-element.232), channel_id=1, source_target_pairs={{4,0},{8,4},{12,8},{16,12},{20,16},{24,20},{28,24},{0,28},{5,1},{9... | collective-permute-start | bytes 786440 | tf_op jit(solution)/shard_map/ppermute | solution.py:17
  90.9 5.1 %collective-permute-done.11 = f32[2,128,256]{2,1,0:T(8,128)S(1)} collective-permute-done((f32[2,128,256]{2,1,0:T(8,128)S(1)}, f32[2,128,256]{2,1,0:T(8,128)S(1)}, u32[]{:S(2)}, u32[]{:S(2)}) %collective-permute-start.11) | collective-permute-done | bytes 262176 | tf_op jit(solution)/shard_map/ppermute | solution.py:17
  96.5 3.8 %shard_map.78.w_in = f32[768,256]{1,0:T(8,128)S(1)} custom-call(s32[6,2]{1,0:T(8,128)S(1)} %copy.15.offs, f32[2,384,256]{2,1,0:T(8,128)S(1)} %multiply_subtract_fusion.2.tall, f32[2,384,128]{2,1,0:T(8,128)S(1)} %collective-permute-done.17.right, f32[2,128,128]{2,1,0:T(8,128)S(1)} %copy-done.1, f32[2,128,128]{2,1,0:T(8,128)S(1)} %pad_maximum_fusion.4.phase, ...), custom_call_target="tpu_custom_call" | custom-call | flops 1207959552 | bytes 6000000 | tf_op jit(solution)/shard_map/pallas_call | solution.py:228
  100.4 3.8 %shard_map.79 = (f32[768,256]{1,0:T(8,128)S(1)}, f32[768,256]{1,0:T(8,128)S(1)}) custom-call(s32[6,2]{1,0:T(8,128)S(1)} %copy.15.offs, f32[2,384,256]{2,1,0:T(8,128)S(1)} %multiply_subtract_fusion.tall, f32[2,384,128]{2,1,0:T(8,128)S(1)} %collective-permute-done.16.right, f32[768,256]{1,0:T(8,128)S(1)} %shard_map.78.w_in, ...), custom_call_target="tpu_custom_call" | custom-call | flops 1207959552 | bytes 6000000 | tf_op jit(solution)/shard_map/pallas_call | solution.py:228
  104.3 4.1 %shard_map.80 = (f32[2,384,256]{2,1,0:T(8,128)S(1)}, f32[2,384,128]{2,1,0:T(8,128)S(1)}, f32[768,256]{1,0:T(8,128)S(1)}) custom-call(s32[6,2]{1,0:T(8,128)S(1)} %copy.15.offs, f32[2,384,256]{2,1,0:T(8,128)S(1)} %multiply_subtract_fusion.1.tall, f32[2,384,128]{2,1,0:T(8,128)S(1)} %collective-permute-done.12.right, f32[768,256]{1,0:T(8,128)S(1)} %get-tuple-element.215.w_in, ...), custom_call_target="tpu_custom_call" | custom-call | flops 1207959552 | bytes 6000000 | tf_op jit(solution)/shard_map/pallas_call | solution.py:228
  108.7 4.0 %shard_map.81 = (f32[2,384,256]{2,1,0:T(8,128)S(1)}, f32[2,384,128]{2,1,0:T(8,128)S(1)}, f32[768,256]{1,0:T(8,128)S(1)}) custom-call(s32[6,2]{1,0:T(8,128)S(1)} %copy.15.offs, f32[768,256]{1,0:T(8,128)S(1)} %get-tuple-element.216.g_in, f32[768,256]{1,0:T(8,128)S(1)} %shard_map.78.w_in, f32[768,256]{1,0:T(8,128)S(1)} %get-tuple-element.217.o_in, ...), custom_call_target="tpu_custom_call" | custom-call | flops 1207959552 | bytes 6000000 | tf_op jit(solution)/shard_map/pallas_call | solution.py:228
  114.2 3.9 %shard_map.82 = (f32[2,384,256]{2,1,0:T(8,128)S(1)}, f32[2,384,128]{2,1,0:T(8,128)S(1)}) custom-call(s32[6,2]{1,0:T(8,128)S(1)} %copy.15.offs, f32[768,256]{1,0:T(8,128)S(1)} %get-tuple-element.218.g_in, f32[2,128,128]{2,1,0:T(8,128)S(1)} %copy-done.1, f32[2,128,128]{2,1,0:T(8,128)S(1)} %pad_maximum_fusion.4.phase, bf16[2,768,256]{2,1,0:T(8,128)(2,1)S(1)} %copy-done.3, ...), custom_call_target="tpu_custom_call" | custom-call | flops 1207959552 | bytes 6000000 | tf_op jit(solution)/shard_map/pallas_call | solution.py:228
  120.4 5.0 %collective-permute-done.18 = f32[2,384,128]{2,1,0:T(8,128)S(1)} collective-permute-done((f32[2,384,128]{2,1,0:T(8,128)S(1)}, f32[2,384,128]{2,1,0:T(8,128)S(1)}, u32[]{:S(2)}, u32[]{:S(2)}) %collective-permute-start.18) | collective-permute-done | bytes 393248 | tf_op jit(solution)/shard_map/ppermute | solution.py:17
  125.7 4.7 %collective-permute-done.23 = f32[2,128,256]{2,1,0:T(8,128)S(1)} collective-permute-done((f32[2,128,256]{2,1,0:T(8,128)S(1)}, f32[2,128,256]{2,1,0:T(8,128)S(1)}, u32[]{:S(2)}, u32[]{:S(2)}) %collective-permute-start.23) | collective-permute-done | bytes 262176 | tf_op jit(solution)/shard_map/ppermute | solution.py:17
  130.5 10.8 %collective-permute-done.21 = f32[2,128,256]{2,1,0:T(8,128)S(1)} collective-permute-done((f32[2,128,256]{2,1,0:T(8,128)S(1)}, f32[2,128,256]{2,1,0:T(8,128)S(1)}, u32[]{:S(2)}, u32[]{:S(2)}) %collective-permute-start.21) | collective-permute-done | bytes 262176 | tf_op jit(solution)/shard_map/ppermute | solution.py:17
  (94 shorter events, 25.2 us)
Async XLA Ops:
  1.5 12.8 %collective-permute-start.3 = (f32[2,128,256]{2,1,0:T(8,128)S(1)}, f32[2,128,256]{2,1,0:T(8,128)S(1)}, u32[]{:S(2)}, u32[]{:S(2)}) collective-permute-start(f32[2,128,256]{2,1,0:T(8,128)S(1)} %slice.481), channel_id=1, source_target_pairs={{4,0},{8,4},{12,8},{16,12},{20,16},{24,20},{28,24},{0,28},{5,1},{9... | collective-permute-start | bytes 786440 | tf_op jit(solution)/shard_map/ppermute | solution.py:17
  7.6 12.3 %collective-permute-start.1 = (f32[2,128,256]{2,1,0:T(8,128)S(1)}, f32[2,128,256]{2,1,0:T(8,128)S(1)}, u32[]{:S(2)}, u32[]{:S(2)}) collective-permute-start(f32[2,128,256]{2,1,0:T(8,128)S(1)} %slice.478), channel_id=1, source_target_pairs={{4,0},{8,4},{12,8},{16,12},{20,16},{24,20},{28,24},{0,28},{5,1},{9... | collective-permute-start | bytes 786440 | tf_op jit(solution)/shard_map/ppermute | solution.py:17
  8.2 16.2 %collective-permute-start = (f32[2,128,256]{2,1,0:T(8,128)S(1)}, f32[2,128,256]{2,1,0:T(8,128)S(1)}, u32[]{:S(2)}, u32[]{:S(2)}) collective-permute-start(f32[2,128,256]{2,1,0:T(8,128)S(1)} %slice.477), channel_id=1, source_target_pairs={{4,0},{8,4},{12,8},{16,12},{20,16},{24,20},{28,24},{0,28},{5,1},{9... | collective-permute-start | bytes 786440 | tf_op jit(solution)/shard_map/ppermute | solution.py:17
  14.3 19.4 %collective-permute-start.4 = (f32[2,384,128]{2,1,0:T(8,128)S(1)}, f32[2,384,128]{2,1,0:T(8,128)S(1)}, u32[]{:S(2)}, u32[]{:S(2)}) collective-permute-start(f32[2,384,128]{2,1,0:T(8,128)S(1)} %fusion.3), channel_id=1, source_target_pairs={{1,0},{2,1},{3,2},{0,3},{5,4},{6,5},{7,6},{4,7},{9,8},{10,9},{11,1... | collective-permute-start | bytes 1179656 | tf_op jit(solution)/shard_map/ppermute | solution.py:17
  19.9 17.6 %collective-permute-start.2 = (f32[2,384,128]{2,1,0:T(8,128)S(1)}, f32[2,384,128]{2,1,0:T(8,128)S(1)}, u32[]{:S(2)}, u32[]{:S(2)}) collective-permute-start(f32[2,384,128]{2,1,0:T(8,128)S(1)} %fusion.4), channel_id=1, source_target_pairs={{1,0},{2,1},{3,2},{0,3},{5,4},{6,5},{7,6},{4,7},{9,8},{10,9},{11,1... | collective-permute-start | bytes 1179656 | tf_op jit(solution)/shard_map/ppermute | solution.py:17
  24.4 5.4 %collective-permute-start.5 = (f32[2,384,128]{2,1,0:T(8,128)S(1)}, f32[2,384,128]{2,1,0:T(8,128)S(1)}, u32[]{:S(2)}, u32[]{:S(2)}) collective-permute-start(f32[2,384,128]{2,1,0:T(8,128)S(1)} %fusion.5), channel_id=1, source_target_pairs={{1,0},{2,1},{3,2},{0,3},{5,4},{6,5},{7,6},{4,7},{9,8},{10,9},{11,1... | collective-permute-start | bytes 1179656 | tf_op jit(solution)/shard_map/ppermute | solution.py:17
  49.6 7.4 %collective-permute-start.6 = (f32[2,384,128]{2,1,0:T(8,128)S(1)}, f32[2,384,128]{2,1,0:T(8,128)S(1)}, u32[]{:S(2)}, u32[]{:S(2)}) collective-permute-start(f32[2,384,128]{2,1,0:T(8,128)S(1)} %get-tuple-element.210), channel_id=1, source_target_pairs={{3,0},{0,1},{1,2},{2,3},{7,4},{4,5},{5,6},{6,7},{11,8},{8,9},{9,10... | collective-permute-start | bytes 1179656 | tf_op jit(solution)/shard_map/ppermute | solution.py:17
  51.4 9.8 %collective-permute-start.13 = (f32[2,384,128]{2,1,0:T(8,128)S(1)}, f32[2,384,128]{2,1,0:T(8,128)S(1)}, u32[]{:S(2)}, u32[]{:S(2)}) collective-permute-start(f32[2,384,128]{2,1,0:T(8,128)S(1)} %get-tuple-element.214), channel_id=1, source_target_pairs={{3,0},{0,1},{1,2},{2,3},{7,4},{4,5},{5,6},{6,7},{11,8},{8,9},{9,10... | collective-permute-start | bytes 1179656 | tf_op jit(solution)/shard_map/ppermute | solution.py:17
  51.5 14.0 %collective-permute-start.9 = (f32[2,384,128]{2,1,0:T(8,128)S(1)}, f32[2,384,128]{2,1,0:T(8,128)S(1)}, u32[]{:S(2)}, u32[]{:S(2)}) collective-permute-start(f32[2,384,128]{2,1,0:T(8,128)S(1)} %get-tuple-element.212), channel_id=1, source_target_pairs={{3,0},{0,1},{1,2},{2,3},{7,4},{4,5},{5,6},{6,7},{11,8},{8,9},{9,10... | collective-permute-start | bytes 1179656 | tf_op jit(solution)/shard_map/ppermute | solution.py:17
  57.2 12.1 %collective-permute-start.7 = (f32[2,128,256]{2,1,0:T(8,128)S(1)}, f32[2,128,256]{2,1,0:T(8,128)S(1)}, u32[]{:S(2)}, u32[]{:S(2)}) collective-permute-start(f32[2,128,256]{2,1,0:T(8,128)S(1)} %slice.487), channel_id=1, source_target_pairs={{28,0},{0,4},{4,8},{8,12},{12,16},{16,20},{20,24},{24,28},{29,1},{... | collective-permute-start | bytes 786440 | tf_op jit(solution)/shard_map/ppermute | solution.py:17
  61.4 16.4 %collective-permute-start.14 = (f32[2,128,256]{2,1,0:T(8,128)S(1)}, f32[2,128,256]{2,1,0:T(8,128)S(1)}, u32[]{:S(2)}, u32[]{:S(2)}) collective-permute-start(f32[2,128,256]{2,1,0:T(8,128)S(1)} %slice.495), channel_id=1, source_target_pairs={{28,0},{0,4},{4,8},{8,12},{12,16},{16,20},{20,24},{24,28},{29,1},{... | collective-permute-start | bytes 786440 | tf_op jit(solution)/shard_map/ppermute | solution.py:17
  65.6 19.6 %collective-permute-start.10 = (f32[2,128,256]{2,1,0:T(8,128)S(1)}, f32[2,128,256]{2,1,0:T(8,128)S(1)}, u32[]{:S(2)}, u32[]{:S(2)}) collective-permute-start(f32[2,128,256]{2,1,0:T(8,128)S(1)} %slice.491), channel_id=1, source_target_pairs={{28,0},{0,4},{4,8},{8,12},{12,16},{16,20},{20,24},{24,28},{29,1},{... | collective-permute-start | bytes 786440 | tf_op jit(solution)/shard_map/ppermute | solution.py:17
  69.4 20.1 %collective-permute-start.8 = (f32[2,128,256]{2,1,0:T(8,128)S(1)}, f32[2,128,256]{2,1,0:T(8,128)S(1)}, u32[]{:S(2)}, u32[]{:S(2)}) collective-permute-start(f32[2,128,256]{2,1,0:T(8,128)S(1)} %get-tuple-element.228), channel_id=1, source_target_pairs={{4,0},{8,4},{12,8},{16,12},{20,16},{24,20},{28,24},{0,28},{5,1},{9... | collective-permute-start | bytes 786440 | tf_op jit(solution)/shard_map/ppermute | solution.py:17
  77.8 12.7 %collective-permute-start.15 = (f32[2,128,256]{2,1,0:T(8,128)S(1)}, f32[2,128,256]{2,1,0:T(8,128)S(1)}, u32[]{:S(2)}, u32[]{:S(2)}) collective-permute-start(f32[2,128,256]{2,1,0:T(8,128)S(1)} %get-tuple-element.230), channel_id=1, source_target_pairs={{4,0},{8,4},{12,8},{16,12},{20,16},{24,20},{28,24},{0,28},{5,1},{9... | collective-permute-start | bytes 786440 | tf_op jit(solution)/shard_map/ppermute | solution.py:17
  85.2 10.8 %collective-permute-start.11 = (f32[2,128,256]{2,1,0:T(8,128)S(1)}, f32[2,128,256]{2,1,0:T(8,128)S(1)}, u32[]{:S(2)}, u32[]{:S(2)}) collective-permute-start(f32[2,128,256]{2,1,0:T(8,128)S(1)} %get-tuple-element.232), channel_id=1, source_target_pairs={{4,0},{8,4},{12,8},{16,12},{20,16},{24,20},{28,24},{0,28},{5,1},{9... | collective-permute-start | bytes 786440 | tf_op jit(solution)/shard_map/ppermute | solution.py:17
  89.7 6.9 %collective-permute-start.17 = (f32[2,384,128]{2,1,0:T(8,128)S(1)}, f32[2,384,128]{2,1,0:T(8,128)S(1)}, u32[]{:S(2)}, u32[]{:S(2)}) collective-permute-start(f32[2,384,128]{2,1,0:T(8,128)S(1)} %slice.498), channel_id=1, source_target_pairs={{1,0},{2,1},{3,2},{0,3},{5,4},{6,5},{7,6},{4,7},{9,8},{10,9},{11,1... | collective-permute-start | bytes 1179656 | tf_op jit(solution)/shard_map/ppermute | solution.py:17
  90.7 9.7 %collective-permute-start.16 = (f32[2,384,128]{2,1,0:T(8,128)S(1)}, f32[2,384,128]{2,1,0:T(8,128)S(1)}, u32[]{:S(2)}, u32[]{:S(2)}) collective-permute-start(f32[2,384,128]{2,1,0:T(8,128)S(1)} %slice.497), channel_id=1, source_target_pairs={{1,0},{2,1},{3,2},{0,3},{5,4},{6,5},{7,6},{4,7},{9,8},{10,9},{11,1... | collective-permute-start | bytes 1179656 | tf_op jit(solution)/shard_map/ppermute | solution.py:17
  96.2 8.0 %collective-permute-start.12 = (f32[2,384,128]{2,1,0:T(8,128)S(1)}, f32[2,384,128]{2,1,0:T(8,128)S(1)}, u32[]{:S(2)}, u32[]{:S(2)}) collective-permute-start(f32[2,384,128]{2,1,0:T(8,128)S(1)} %slice.493), channel_id=1, source_target_pairs={{1,0},{2,1},{3,2},{0,3},{5,4},{6,5},{7,6},{4,7},{9,8},{10,9},{11,1... | collective-permute-start | bytes 1179656 | tf_op jit(solution)/shard_map/ppermute | solution.py:17
  108.4 9.9 %collective-permute-start.22 = (f32[2,384,128]{2,1,0:T(8,128)S(1)}, f32[2,384,128]{2,1,0:T(8,128)S(1)}, u32[]{:S(2)}, u32[]{:S(2)}) collective-permute-start(f32[2,384,128]{2,1,0:T(8,128)S(1)} %get-tuple-element.224), channel_id=1, source_target_pairs={{3,0},{0,1},{1,2},{2,3},{7,4},{4,5},{5,6},{6,7},{11,8},{8,9},{9,10... | collective-permute-start | bytes 1179656 | tf_op jit(solution)/shard_map/ppermute | solution.py:17
  112.7 7.5 %collective-permute-start.20 = (f32[2,384,128]{2,1,0:T(8,128)S(1)}, f32[2,384,128]{2,1,0:T(8,128)S(1)}, u32[]{:S(2)}, u32[]{:S(2)}) collective-permute-start(f32[2,384,128]{2,1,0:T(8,128)S(1)} %get-tuple-element.222), channel_id=1, source_target_pairs={{3,0},{0,1},{1,2},{2,3},{7,4},{4,5},{5,6},{6,7},{11,8},{8,9},{9,10... | collective-permute-start | bytes 1179656 | tf_op jit(solution)/shard_map/ppermute | solution.py:17
  118.1 7.3 %collective-permute-start.18 = (f32[2,384,128]{2,1,0:T(8,128)S(1)}, f32[2,384,128]{2,1,0:T(8,128)S(1)}, u32[]{:S(2)}, u32[]{:S(2)}) collective-permute-start(f32[2,384,128]{2,1,0:T(8,128)S(1)} %get-tuple-element.220), channel_id=1, source_target_pairs={{3,0},{0,1},{1,2},{2,3},{7,4},{4,5},{5,6},{6,7},{11,8},{8,9},{9,10... | collective-permute-start | bytes 1179656 | tf_op jit(solution)/shard_map/ppermute | solution.py:17
  118.4 11.9 %collective-permute-start.23 = (f32[2,128,256]{2,1,0:T(8,128)S(1)}, f32[2,128,256]{2,1,0:T(8,128)S(1)}, u32[]{:S(2)}, u32[]{:S(2)}) collective-permute-start(f32[2,128,256]{2,1,0:T(8,128)S(1)} %slice.509), channel_id=1, source_target_pairs={{28,0},{0,4},{4,8},{8,12},{12,16},{16,20},{20,24},{24,28},{29,1},{... | collective-permute-start | bytes 786440 | tf_op jit(solution)/shard_map/ppermute | solution.py:17
  125.6 15.8 %collective-permute-start.19 = (f32[2,128,256]{2,1,0:T(8,128)S(1)}, f32[2,128,256]{2,1,0:T(8,128)S(1)}, u32[]{:S(2)}, u32[]{:S(2)}) collective-permute-start(f32[2,128,256]{2,1,0:T(8,128)S(1)} %slice.501), channel_id=1, source_target_pairs={{28,0},{0,4},{4,8},{8,12},{12,16},{16,20},{20,24},{24,28},{29,1},{... | collective-permute-start | bytes 786440 | tf_op jit(solution)/shard_map/ppermute | solution.py:17
  125.6 15.7 %collective-permute-start.21 = (f32[2,128,256]{2,1,0:T(8,128)S(1)}, f32[2,128,256]{2,1,0:T(8,128)S(1)}, u32[]{:S(2)}, u32[]{:S(2)}) collective-permute-start(f32[2,128,256]{2,1,0:T(8,128)S(1)} %slice.505), channel_id=1, source_target_pairs={{28,0},{0,4},{4,8},{8,12},{12,16},{16,20},{20,24},{24,28},{29,1},{... | collective-permute-start | bytes 786440 | tf_op jit(solution)/shard_map/ppermute | solution.py:17
  (6 other events, 36.2 us)
where the time goes:
time: 143 us
  waiting for transfers between devices  69.4 us (49%)
  Pallas kernels  39.5 us (28%)
  starting transfers between devices  28.2 us (20%)
  local copies, waits for them, and re-layouts  3.43 us (2%)
  other arithmetic  1.85 us (1%)
    ppermute x24, waiting for transfers between devices, passed_along(): lax.ppermute(block, axis, [((i - distance) % n, i) for i in range(n)])  69.4 us
    pallas_call x10, Pallas kernels, call(): pl.pallas_call(body, out_shape=outs, in_specs=[pl.BlockSpec(memory_space=...  39.5 us
    ppermute x24, starting transfers between devices, passed_along(): lax.ppermute(block, axis, [((i - distance) % n, i) for i in range(n)])  28.2 us
  transfers between devices with their start and end apart: 24, of which 15 were waited for; matrix products, arithmetic and copies ran while one was open for 2% of the time, Pallas kernels for 16%

commit v1 on v0

--- a/solution.py
+++ b/solution.py
@@ -17,6 +17,10 @@
     return lax.ppermute(block, axis, [((i - distance) % n, i) for i in range(n)])
 
 
+def after(value, *others):
+    return lax.optimization_barrier((value, *others))[0] if others else value
+
+
 def tables(h):
     k = np.arange(h)
     angle = (k[:, None] * k[None, :] % h) * (-2.0 * np.pi / h)
@@ -29,9 +33,7 @@
 
     ah, al = halves(np.block([[c, s], [-s, c]]))
     bh, bl = halves(np.block([[c, -s], [s, c]]))
-    right = [np.concatenate([x, x, y], 0) for x, y in ((ah, al), (bh, bl))]
-    left = [np.concatenate([x, x, y], 1) for x, y in ((bh, bl), (ah, al))]
-    return np.stack(right), np.stack(left)
+    return np.stack([ah, bh]), np.stack([al, bl])
 
 
 def split(x):
@@ -132,7 +134,8 @@
 
 
 def tab_of(tr, tl):
-    return ([tr[0], tr[1]], [tl[0], tl[1]])
+    pairs = [(tr[i], tl[i]) for i in range(2)]
+    return ([jnp.concatenate([x, x, y], 0) for x, y in pairs], [jnp.concatenate([x, x, y], 1) for x, y in pairs[::-1]])
 
 
 def rows_of(ps, h):
@@ -220,7 +223,7 @@
     wave = jax.ShapeDtypeStruct((pos * h, 2 * h), F32)
     ext = pltpu.VMEM((2, tile_r + h, tile_c + h), F32)
     grad = [jax.ShapeDtypeStruct((2, tile_r + h, tile_c), F32), jax.ShapeDtypeStruct((2, tile_r + h, h), F32)]
-    flops = 2 * 2 * 2 * 3 * pos * h * (2 * h) ** 2
+    flops = 8 * 2 * 2 * 2 * 3 * pos * h * (2 * h) ** 2
     cost = pl.CostEstimate(flops=flops, bytes_accessed=6_000_000, transcendentals=0)
 
     def call(body, outs, scratch, *args):
@@ -235,15 +238,21 @@
             compiler_params=pltpu.CompilerParams(vmem_limit_bytes=40 * 1024 * 1024),
         )(offs, *args)
 
-    tall, right = [], []
-    for s in range(slices):
-        own = object_field[:, s]
-        tall.append(jnp.concatenate([own, passed_along(own[:, :h], "row", -1)], 1))
-    for s in range(slices):
-        right.append(passed_along(tall[s][:, :, :h], "col", -1))
+    first, rest = object_field[:, 0], object_field[:, 1:].reshape(2 * slices - 2, tile_r, tile_c)
+    tall_first = jnp.concatenate([first, passed_along(first[:, :h], "row", -1)], 1)
+    tall_rest = jnp.concatenate([rest, passed_along(rest[:, :h], "row", -1)], 1)
+    right_first = passed_along(tall_first[:, :, :h], "col", -1)
+    right_rest = passed_along(tall_rest[:, :, :h], "col", -1)
+
+    def layers(one, others):
+        others = others.reshape(2, slices - 1, *others.shape[1:])
+        return [one] + [others[:, s] for s in range(slices - 1)]
+
+    tall, right = layers(after(tall_first, tall_rest), tall_rest), layers(right_first, right_rest)
 
     result = [None] * slices
     for step in range(ITERS):
+        last = step + 1 == ITERS
         waves, objects = [None], [None]
         (w,) = call(k_first, [wave], [ext], tall[0], right[0], probe, phase, tr, tl)
         waves.append(w)
@@ -252,20 +261,34 @@
             waves.append(w)
             objects.append(o)
         s = slices - 1
-        grads = [None] * slices
-        *grads[s], g = call(k_last, grad + [wave], [ext, ext], tall[s], right[s], waves[s], target, tr, tl)
-        for s in range(slices - 2, 0, -1):
-            *grads[s], g = call(k_back, grad + [wave], [ext], g, waves[s], objects[s], phase, tr, tl)
-        grads[0] = call(k_back_first, grad, [ext], g, probe, phase, tr, tl)
-        last = step + 1 == ITERS
-        for s in range(slices - 1, -1, -1):
-            gl, gr = grads[s]
-            total = gl.at[:, :, :h].add(passed_along(gr, "col", 1))
+        totals = [None] * slices
+
+        def widened(gl, gr):
+            return gl.at[:, :, :h].add(passed_along(gr, "col", 1))
+
+        gl, gr, g = call(k_last, grad + [wave], [ext, ext], tall[s], right[s], waves[s], target, tr, tl)
+        totals[s] = widened(gl, gr)
+        for s in range(slices - 2, -1, -1):
+            if s + 2 < slices:
+                g = after(g, totals[s + 2])
+            if s:
+                gl, gr, g = call(k_back, grad + [wave], [ext], g, waves[s], objects[s], phase, tr, tl)
+            else:
+                gl, gr = call(k_back_first, grad, [ext], g, probe, phase, tr, tl)
+            totals[s] = widened(gl, gr)
+        order = list(range(slices - 1, -1, -1))
+        if not last:
+            order = order[:1] + order[-1:] + order[1:-1]
+        earlier = ()
+        for s in order:
+            total = after(totals[s], *earlier)
             above = passed_along(total[:, tile_r:], "row", 1)
+            earlier = (above,)
             if last:
                 result[s] = tall[s][:, :tile_r] - STEP * total[:, :tile_r].at[:, :h].add(above)
             else:
                 below = passed_along(total[:, :h], "row", -1)
+                earlier = (above, below)
                 total = total.at[:, :h].add(above).at[:, tile_r:].add(below)
                 tall[s] = tall[s] - STEP * total
                 right[s] = passed_along(tall[s][:, :, :h], "col", -1)

time: 143 us -> 150 us (1.049)
  waiting for transfers between devices: 69.4 us -> 86 us
  starting transfers between devices: 28.2 us -> 16.6 us
  local copies, waits for them, and re-layouts: 3.43 us -> 5.35 us
    ppermute x24 -> x22, waiting for transfers between devices: 69.4 us -> 86 us  [passed_along(): lax.ppermute(block, axis, [((i - distance) % n, i) for i in range(n)])]
    ppermute x24 -> x22, starting transfers between devices: 28.2 us -> 16.6 us  [passed_along(): lax.ppermute(block, axis, [((i - distance) % n, i) for i in range(n)])]
  transfers between devices with their start and end apart: 24 -> 22, of which waited for: 15 -> 17; matrix products, arithmetic and copies ran while one was open for 2% -> 2% of each run, Pallas kernels for 16% -> 18%
where the time goes in v1:
time: 150 us
  waiting for transfers between devices  86 us (57%)
  Pallas kernels  39.4 us (26%)
  starting transfers between devices  16.6 us (11%)
  local copies, waits for them, and re-layouts  5.35 us (4%)
  other arithmetic  1.85 us (1%)
    ppermute x22, waiting for transfers between devices, passed_along(): lax.ppermute(block, axis, [((i - distance) % n, i) for i in range(n)])  86 us
    pallas_call x10, Pallas kernels, call(): pl.pallas_call(body, out_shape=outs, in_specs=[pl.BlockSpec(memory_space=...  39.4 us
    ppermute x22, starting transfers between devices, passed_along(): lax.ppermute(block, axis, [((i - distance) % n, i) for i in range(n)])  16.6 us
  transfers between devices with their start and end apart: 22, of which 17 were waited for; matrix products, arithmetic and copies ran while one was open for 2% of the time, Pallas kernels for 18%

profile of v1, /device:TPU:0, one launch (start us, length us, event | category | flops | bytes accessed | tf_op | source)
XLA Modules:
  0.0 149.6 jit_solution(17423365438918508464)
XLA Ops:
  1.1 6.1 %collective-permute-start = (f32[2,128,256]{2,1,0:T(8,128)S(1)}, f32[2,128,256]{2,1,0:T(8,128)S(1)}, u32[]{:S(2)}, u32[]{:S(2)}) collective-permute-start(f32[2,128,256]{2,1,0:T(8,128)S(1)} %slice.481), channel_id=1, source_target_pairs={{4,0},{8,4},{12,8},{16,12},{20,16},{24,20},{28,24},{0,28},{5,1},{9... | collective-permute-start | bytes 786440 | tf_op jit(solution)/shard_map/ppermute | solution.py:17
  9.5 4.4 %collective-permute-done = f32[2,128,256]{2,1,0:T(8,128)S(1)} collective-permute-done((f32[2,128,256]{2,1,0:T(8,128)S(1)}, f32[2,128,256]{2,1,0:T(8,128)S(1)}, u32[]{:S(2)}, u32[]{:S(2)}) %collective-permute-start) | collective-permute-done | bytes 262176 | tf_op jit(solution)/shard_map/ppermute | solution.py:17
  14.1 9.9 %collective-permute-done.1 = f32[4,128,256]{2,1,0:T(8,128)S(1)} collective-permute-done((f32[4,128,256]{2,1,0:T(8,128)S(1)}, f32[4,128,256]{2,1,0:T(8,128)S(1)}, u32[]{:S(2)}, u32[]{:S(2)}) %collective-permute-start.1) | collective-permute-done | bytes 524320 | tf_op jit(solution)/shard_map/ppermute | solution.py:17
  25.3 3.8 %shard_map.73.w_in = f32[768,256]{1,0:T(8,128)S(1)} custom-call(s32[6,2]{1,0:T(8,128)S(1)} %copy.31.offs, f32[2,384,256]{2,1,0:T(8,128)S(1)} %pad_maximum_fusion.2.tall, f32[2,384,128]{2,1,0:T(8,128)S(1)} %collective-permute-done.3.right, f32[2,128,128]{2,1,0:T(8,128)S(1)} %copy-done.1, f32[2,128,128]{2,1,0:T(8,128)S(1)} %pad_maximum_fusion.4.phase, ...), custom_call_target="tpu_custom_call" | custom-call | flops 9663676416 | bytes 6000000 | tf_op jit(solution)/shard_map/pallas_call | solution.py:231
  29.1 4.6 %collective-permute-done.2 = f32[4,384,128]{2,1,0:T(8,128)S(1)} collective-permute-done((f32[4,384,128]{2,1,0:T(8,128)S(1)}, f32[4,384,128]{2,1,0:T(8,128)S(1)}, u32[]{:S(2)}, u32[]{:S(2)}) %collective-permute-start.2) | collective-permute-done | bytes 786464 | tf_op jit(solution)/shard_map/ppermute | solution.py:17
  33.7 3.8 %shard_map.74 = (f32[768,256]{1,0:T(8,128)S(1)}, f32[768,256]{1,0:T(8,128)S(1)}) custom-call(s32[6,2]{1,0:T(8,128)S(1)} %copy.31.offs, f32[2,384,256]{2,1,0:T(8,128)S(1)} %get-tuple-element.239.tall, f32[2,384,128]{2,1,0:T(8,128)S(1)} %get-tuple-element.247.right, f32[768,256]{1,0:T(8,128)S(1)} %shard_map.73.w_in, ...), custom_call_target="tpu_custom_call" | custom-call | flops 9663676416 | bytes 6000000 | tf_op jit(solution)/shard_map/pallas_call | solution.py:231
  37.6 4.1 %shard_map.75 = (f32[2,384,256]{2,1,0:T(8,128)S(1)}, f32[2,384,128]{2,1,0:T(8,128)S(1)}, f32[768,256]{1,0:T(8,128)S(1)}) custom-call(s32[6,2]{1,0:T(8,128)S(1)} %copy.31.offs, f32[2,384,256]{2,1,0:T(8,128)S(1)} %get-tuple-element.240.tall, f32[2,384,128]{2,1,0:T(8,128)S(1)} %get-tuple-element.248.right, f32[768,256]{1,0:T(8,128)S(1)} %get-tuple-element.213.w_in, ...), custom_call_target="tpu_custom_call" | custom-call | flops 9663676416 | bytes 6000000 | tf_op jit(solution)/shard_map/pallas_call | solution.py:231
  43.5 4.0 %shard_map.76 = (f32[2,384,256]{2,1,0:T(8,128)S(1)}, f32[2,384,128]{2,1,0:T(8,128)S(1)}, f32[768,256]{1,0:T(8,128)S(1)}) custom-call(s32[6,2]{1,0:T(8,128)S(1)} %copy.31.offs, f32[768,256]{1,0:T(8,128)S(1)} %get-tuple-element.214.g_in, f32[768,256]{1,0:T(8,128)S(1)} %shard_map.73.w_in, f32[768,256]{1,0:T(8,128)S(1)} %get-tuple-element.215.o_in, ...), custom_call_target="tpu_custom_call" | custom-call | flops 9663676416 | bytes 6000000 | tf_op jit(solution)/shard_map/pallas_call | solution.py:231
  49.9 3.9 %shard_map.77 = (f32[2,384,256]{2,1,0:T(8,128)S(1)}, f32[2,384,128]{2,1,0:T(8,128)S(1)}) custom-call(s32[6,2]{1,0:T(8,128)S(1)} %copy.31.offs, f32[768,256]{1,0:T(8,128)S(1)} %get-tuple-element.219.g_in, f32[2,128,128]{2,1,0:T(8,128)S(1)} %copy-done.1, f32[2,128,128]{2,1,0:T(8,128)S(1)} %pad_maximum_fusion.4.phase, bf16[2,256,256]{2,1,0:T(8,128)(2,1)S(1)} %copy-done.3, ...), custom_call_target="tpu_custom_call" | custom-call | flops 9663676416 | bytes 6000000 | tf_op jit(solution)/shard_map/pallas_call | solution.py:231
  53.9 6.3 %collective-permute-done.6 = f32[2,128,256]{2,1,0:T(8,128)S(1)} collective-permute-done((f32[2,128,256]{2,1,0:T(8,128)S(1)}, f32[2,128,256]{2,1,0:T(8,128)S(1)}, u32[]{:S(2)}, u32[]{:S(2)}) %collective-permute-start.6) | collective-permute-done | bytes 262176 | tf_op jit(solution)/shard_map/ppermute | solution.py:17
  62.2 4.8 %collective-permute-done.7 = f32[2,128,256]{2,1,0:T(8,128)S(1)} collective-permute-done((f32[2,128,256]{2,1,0:T(8,128)S(1)}, f32[2,128,256]{2,1,0:T(8,128)S(1)}, u32[]{:S(2)}, u32[]{:S(2)}) %collective-permute-start.7) | collective-permute-done | bytes 262176 | tf_op jit(solution)/shard_map/ppermute | solution.py:17
  67.1 9.1 %collective-permute-done.8 = f32[2,128,256]{2,1,0:T(8,128)S(1)} collective-permute-done((f32[2,128,256]{2,1,0:T(8,128)S(1)}, f32[2,128,256]{2,1,0:T(8,128)S(1)}, u32[]{:S(2)}, u32[]{:S(2)}) %collective-permute-start.8) | collective-permute-done | bytes 262176 | tf_op jit(solution)/shard_map/ppermute | solution.py:17
  78.0 4.7 %collective-permute-done.9 = f32[2,128,256]{2,1,0:T(8,128)S(1)} collective-permute-done((f32[2,128,256]{2,1,0:T(8,128)S(1)}, f32[2,128,256]{2,1,0:T(8,128)S(1)}, u32[]{:S(2)}, u32[]{:S(2)}) %collective-permute-start.9) | collective-permute-done | bytes 262176 | tf_op jit(solution)/shard_map/ppermute | solution.py:17
  83.1 8.9 %collective-permute-done.12 = f32[2,128,256]{2,1,0:T(8,128)S(1)} collective-permute-done((f32[2,128,256]{2,1,0:T(8,128)S(1)}, f32[2,128,256]{2,1,0:T(8,128)S(1)}, u32[]{:S(2)}, u32[]{:S(2)}) %collective-permute-start.12) | collective-permute-done | bytes 262176 | tf_op jit(solution)/shard_map/ppermute | solution.py:17
  93.8 4.7 %collective-permute-done.13 = f32[2,128,256]{2,1,0:T(8,128)S(1)} collective-permute-done((f32[2,128,256]{2,1,0:T(8,128)S(1)}, f32[2,128,256]{2,1,0:T(8,128)S(1)}, u32[]{:S(2)}, u32[]{:S(2)}) %collective-permute-start.13) | collective-permute-done | bytes 262176 | tf_op jit(solution)/shard_map/ppermute | solution.py:17
  99.1 3.8 %shard_map.78.w_in = f32[768,256]{1,0:T(8,128)S(1)} custom-call(s32[6,2]{1,0:T(8,128)S(1)} %copy.31.offs, f32[2,384,256]{2,1,0:T(8,128)S(1)} %multiply_subtract_fusion.2.tall, f32[2,384,128]{2,1,0:T(8,128)S(1)} %collective-permute-done.15.right, f32[2,128,128]{2,1,0:T(8,128)S(1)} %copy-done.1, f32[2,128,128]{2,1,0:T(8,128)S(1)} %pad_maximum_fusion.4.phase, ...), custom_call_target="tpu_custom_call" | custom-call | flops 9663676416 | bytes 6000000 | tf_op jit(solution)/shard_map/pallas_call | solution.py:231
  104.0 3.8 %shard_map.79 = (f32[768,256]{1,0:T(8,128)S(1)}, f32[768,256]{1,0:T(8,128)S(1)}) custom-call(s32[6,2]{1,0:T(8,128)S(1)} %copy.31.offs, f32[2,384,256]{2,1,0:T(8,128)S(1)} %multiply_subtract_fusion.tall, f32[2,384,128]{2,1,0:T(8,128)S(1)} %collective-permute-done.14.right, f32[768,256]{1,0:T(8,128)S(1)} %shard_map.78.w_in, ...), custom_call_target="tpu_custom_call" | custom-call | flops 9663676416 | bytes 6000000 | tf_op jit(solution)/shard_map/pallas_call | solution.py:231
  107.9 4.1 %shard_map.80 = (f32[2,384,256]{2,1,0:T(8,128)S(1)}, f32[2,384,128]{2,1,0:T(8,128)S(1)}, f32[768,256]{1,0:T(8,128)S(1)}) custom-call(s32[6,2]{1,0:T(8,128)S(1)} %copy.31.offs, f32[2,384,256]{2,1,0:T(8,128)S(1)} %multiply_subtract_fusion.1.tall, f32[2,384,128]{2,1,0:T(8,128)S(1)} %collective-permute-done.10.right, f32[768,256]{1,0:T(8,128)S(1)} %get-tuple-element.226.w_in, ...), custom_call_target="tpu_custom_call" | custom-call | flops 9663676416 | bytes 6000000 | tf_op jit(solution)/shard_map/pallas_call | solution.py:231
  112.9 4.0 %shard_map.81 = (f32[2,384,256]{2,1,0:T(8,128)S(1)}, f32[2,384,128]{2,1,0:T(8,128)S(1)}, f32[768,256]{1,0:T(8,128)S(1)}) custom-call(s32[6,2]{1,0:T(8,128)S(1)} %copy.31.offs, f32[768,256]{1,0:T(8,128)S(1)} %get-tuple-element.227.g_in, f32[768,256]{1,0:T(8,128)S(1)} %shard_map.78.w_in, f32[768,256]{1,0:T(8,128)S(1)} %get-tuple-element.228.o_in, ...), custom_call_target="tpu_custom_call" | custom-call | flops 9663676416 | bytes 6000000 | tf_op jit(solution)/shard_map/pallas_call | solution.py:231
  117.0 2.7 %collective-permute-done.16 = f32[2,384,128]{2,1,0:T(8,128)S(1)} collective-permute-done((f32[2,384,128]{2,1,0:T(8,128)S(1)}, f32[2,384,128]{2,1,0:T(8,128)S(1)}, u32[]{:S(2)}, u32[]{:S(2)}) %collective-permute-start.16) | collective-permute-done | bytes 393248 | tf_op jit(solution)/shard_map/ppermute | solution.py:17
  120.8 3.9 %shard_map.82 = (f32[2,384,256]{2,1,0:T(8,128)S(1)}, f32[2,384,128]{2,1,0:T(8,128)S(1)}) custom-call(s32[6,2]{1,0:T(8,128)S(1)} %copy.31.offs, f32[768,256]{1,0:T(8,128)S(1)} %get-tuple-element.232.g_in, f32[2,128,128]{2,1,0:T(8,128)S(1)} %copy-done.1, f32[2,128,128]{2,1,0:T(8,128)S(1)} %pad_maximum_fusion.4.phase, bf16[2,256,256]{2,1,0:T(8,128)(2,1)S(1)} %copy-done.3, ...), custom_call_target="tpu_custom_call" | custom-call | flops 9663676416 | bytes 6000000 | tf_op jit(solution)/shard_map/pallas_call | solution.py:231
  124.9 4.9 %collective-permute-done.19 = f32[2,128,256]{2,1,0:T(8,128)S(1)} collective-permute-done((f32[2,128,256]{2,1,0:T(8,128)S(1)}, f32[2,128,256]{2,1,0:T(8,128)S(1)}, u32[]{:S(2)}, u32[]{:S(2)}) %collective-permute-start.19) | collective-permute-done | bytes 262176 | tf_op jit(solution)/shard_map/ppermute | solution.py:17
  132.1 6.9 %collective-permute-done.20 = f32[2,128,256]{2,1,0:T(8,128)S(1)} collective-permute-done((f32[2,128,256]{2,1,0:T(8,128)S(1)}, f32[2,128,256]{2,1,0:T(8,128)S(1)}, u32[]{:S(2)}, u32[]{:S(2)}) %collective-permute-start.20) | collective-permute-done | bytes 262176 | tf_op jit(solution)/shard_map/ppermute | solution.py:17
  139.2 8.9 %collective-permute-done.21 = f32[2,128,256]{2,1,0:T(8,128)S(1)} collective-permute-done((f32[2,128,256]{2,1,0:T(8,128)S(1)}, f32[2,128,256]{2,1,0:T(8,128)S(1)}, u32[]{:S(2)}, u32[]{:S(2)}) %collective-permute-start.21) | collective-permute-done | bytes 262176 | tf_op jit(solution)/shard_map/ppermute | solution.py:17
  (89 shorter events, 22.8 us)
Async XLA Ops:
  1.1 8.0 %copy-start.5 = (s32[1,1,6,2]{2,3,1,0:T(2,128)S(1)}, s32[1,1,6,2]{2,3,1,0:T(2,128)}, u32[]{:S(2)}) copy-start(s32[1,1,6,2]{2,3,1,0:T(2,128)} %param.41) | copy-start | bytes 148
  1.1 8.1 %copy-start.4 = (f32[128,128]{1,0:T(8,128)S(1)}, f32[128,128]{1,0:T(8,128)}, u32[]{:S(2)}) copy-start(f32[128,128]{1,0:T(8,128)} %param.39) | copy-start | bytes 196612
  1.1 12.8 %collective-permute-start = (f32[2,128,256]{2,1,0:T(8,128)S(1)}, f32[2,128,256]{2,1,0:T(8,128)S(1)}, u32[]{:S(2)}, u32[]{:S(2)}) collective-permute-start(f32[2,128,256]{2,1,0:T(8,128)S(1)} %slice.481), channel_id=1, source_target_pairs={{4,0},{8,4},{12,8},{16,12},{20,16},{24,20},{28,24},{0,28},{5,1},{9... | collective-permute-start | bytes 786440 | tf_op jit(solution)/shard_map/ppermute | solution.py:17
  8.5 15.5 %collective-permute-start.1 = (f32[4,128,256]{2,1,0:T(8,128)S(1)}, f32[4,128,256]{2,1,0:T(8,128)S(1)}, u32[]{:S(2)}, u32[]{:S(2)}) collective-permute-start(f32[4,128,256]{2,1,0:T(8,128)S(1)} %slice.482), channel_id=1, source_target_pairs={{4,0},{8,4},{12,8},{16,12},{20,16},{24,20},{28,24},{0,28},{5,1},{9... | collective-permute-start | bytes 1572872 | tf_op jit(solution)/shard_map/ppermute | solution.py:17
  13.9 10.3 %collective-permute-start.3 = (f32[2,384,128]{2,1,0:T(8,128)S(1)}, f32[2,384,128]{2,1,0:T(8,128)S(1)}, u32[]{:S(2)}, u32[]{:S(2)}) collective-permute-start(f32[2,384,128]{2,1,0:T(8,128)S(1)} %fusion.7), channel_id=1, source_target_pairs={{1,0},{2,1},{3,2},{0,3},{5,4},{6,5},{7,6},{4,7},{9,8},{10,9},{11,1... | collective-permute-start | bytes 1179656 | tf_op jit(solution)/shard_map/ppermute | solution.py:17
  24.0 9.6 %collective-permute-start.2 = (f32[4,384,128]{2,1,0:T(8,128)S(1)}, f32[4,384,128]{2,1,0:T(8,128)S(1)}, u32[]{:S(2)}, u32[]{:S(2)}) collective-permute-start(f32[4,384,128]{2,1,0:T(8,128)S(1)} %fusion.2), channel_id=1, source_target_pairs={{1,0},{2,1},{3,2},{0,3},{5,4},{6,5},{7,6},{4,7},{9,8},{10,9},{11,1... | collective-permute-start | bytes 2359304 | tf_op jit(solution)/shard_map/ppermute | solution.py:17
  41.7 7.4 %collective-permute-start.4 = (f32[2,384,128]{2,1,0:T(8,128)S(1)}, f32[2,384,128]{2,1,0:T(8,128)S(1)}, u32[]{:S(2)}, u32[]{:S(2)}) collective-permute-start(f32[2,384,128]{2,1,0:T(8,128)S(1)} %get-tuple-element.218), channel_id=1, source_target_pairs={{3,0},{0,1},{1,2},{2,3},{7,4},{4,5},{5,6},{6,7},{11,8},{8,9},{9,10... | collective-permute-start | bytes 1179656 | tf_op jit(solution)/shard_map/ppermute | solution.py:17
  49.3 10.9 %collective-permute-start.6 = (f32[2,128,256]{2,1,0:T(8,128)S(1)}, f32[2,128,256]{2,1,0:T(8,128)S(1)}, u32[]{:S(2)}, u32[]{:S(2)}) collective-permute-start(f32[2,128,256]{2,1,0:T(8,128)S(1)} %slice.491), channel_id=1, source_target_pairs={{28,0},{0,4},{4,8},{8,12},{12,16},{16,20},{20,24},{24,28},{29,1},{... | collective-permute-start | bytes 786440 | tf_op jit(solution)/shard_map/ppermute | solution.py:17
  53.8 8.3 %collective-permute-start.5 = (f32[2,384,128]{2,1,0:T(8,128)S(1)}, f32[2,384,128]{2,1,0:T(8,128)S(1)}, u32[]{:S(2)}, u32[]{:S(2)}) collective-permute-start(f32[2,384,128]{2,1,0:T(8,128)S(1)} %get-tuple-element.221), channel_id=1, source_target_pairs={{3,0},{0,1},{1,2},{2,3},{7,4},{4,5},{5,6},{6,7},{11,8},{8,9},{9,10... | collective-permute-start | bytes 1179656 | tf_op jit(solution)/shard_map/ppermute | solution.py:17
  60.3 6.7 %collective-permute-start.7 = (f32[2,128,256]{2,1,0:T(8,128)S(1)}, f32[2,128,256]{2,1,0:T(8,128)S(1)}, u32[]{:S(2)}, u32[]{:S(2)}) collective-permute-start(f32[2,128,256]{2,1,0:T(8,128)S(1)} %get-tuple-element.245), channel_id=1, source_target_pairs={{4,0},{8,4},{12,8},{16,12},{20,16},{24,20},{28,24},{0,28},{5,1},{9... | collective-permute-start | bytes 786440 | tf_op jit(solution)/shard_map/ppermute | solution.py:17
  67.0 9.2 %collective-permute-start.8 = (f32[2,128,256]{2,1,0:T(8,128)S(1)}, f32[2,128,256]{2,1,0:T(8,128)S(1)}, u32[]{:S(2)}, u32[]{:S(2)}) collective-permute-start(f32[2,128,256]{2,1,0:T(8,128)S(1)} %slice.456), channel_id=1, source_target_pairs={{28,0},{0,4},{4,8},{8,12},{12,16},{16,20},{20,24},{24,28},{29,1},{... | collective-permute-start | bytes 786440 | tf_op jit(solution)/shard_map/ppermute | solution.py:17
  67.1 10.8 %collective-permute-start.11 = (f32[2,384,128]{2,1,0:T(8,128)S(1)}, f32[2,384,128]{2,1,0:T(8,128)S(1)}, u32[]{:S(2)}, u32[]{:S(2)}) collective-permute-start(f32[2,384,128]{2,1,0:T(8,128)S(1)} %get-tuple-element.224), channel_id=1, source_target_pairs={{3,0},{0,1},{1,2},{2,3},{7,4},{4,5},{5,6},{6,7},{11,8},{8,9},{9,10... | collective-permute-start | bytes 1179656 | tf_op jit(solution)/shard_map/ppermute | solution.py:17
  76.3 6.4 %collective-permute-start.9 = (f32[2,128,256]{2,1,0:T(8,128)S(1)}, f32[2,128,256]{2,1,0:T(8,128)S(1)}, u32[]{:S(2)}, u32[]{:S(2)}) collective-permute-start(f32[2,128,256]{2,1,0:T(8,128)S(1)} %get-tuple-element.242), channel_id=1, source_target_pairs={{4,0},{8,4},{12,8},{16,12},{20,16},{24,20},{28,24},{0,28},{5,1},{9... | collective-permute-start | bytes 786440 | tf_op jit(solution)/shard_map/ppermute | solution.py:17
  82.7 9.2 %collective-permute-start.12 = (f32[2,128,256]{2,1,0:T(8,128)S(1)}, f32[2,128,256]{2,1,0:T(8,128)S(1)}, u32[]{:S(2)}, u32[]{:S(2)}) collective-permute-start(f32[2,128,256]{2,1,0:T(8,128)S(1)} %slice.463), channel_id=1, source_target_pairs={{28,0},{0,4},{4,8},{8,12},{12,16},{16,20},{20,24},{24,28},{29,1},{... | collective-permute-start | bytes 786440 | tf_op jit(solution)/shard_map/ppermute | solution.py:17
  83.0 24.9 %collective-permute-start.10 = (f32[2,384,128]{2,1,0:T(8,128)S(1)}, f32[2,384,128]{2,1,0:T(8,128)S(1)}, u32[]{:S(2)}, u32[]{:S(2)}) collective-permute-start(f32[2,384,128]{2,1,0:T(8,128)S(1)} %slice.496), channel_id=1, source_target_pairs={{1,0},{2,1},{3,2},{0,3},{5,4},{6,5},{7,6},{4,7},{9,8},{10,9},{11,1... | collective-permute-start | bytes 1179656 | tf_op jit(solution)/shard_map/ppermute | solution.py:17
  92.0 6.4 %collective-permute-start.13 = (f32[2,128,256]{2,1,0:T(8,128)S(1)}, f32[2,128,256]{2,1,0:T(8,128)S(1)}, u32[]{:S(2)}, u32[]{:S(2)}) collective-permute-start(f32[2,128,256]{2,1,0:T(8,128)S(1)} %get-tuple-element.243), channel_id=1, source_target_pairs={{4,0},{8,4},{12,8},{16,12},{20,16},{24,20},{28,24},{0,28},{5,1},{9... | collective-permute-start | bytes 786440 | tf_op jit(solution)/shard_map/ppermute | solution.py:17
  93.7 5.4 %collective-permute-start.15 = (f32[2,384,128]{2,1,0:T(8,128)S(1)}, f32[2,384,128]{2,1,0:T(8,128)S(1)}, u32[]{:S(2)}, u32[]{:S(2)}) collective-permute-start(f32[2,384,128]{2,1,0:T(8,128)S(1)} %slice.499), channel_id=1, source_target_pairs={{1,0},{2,1},{3,2},{0,3},{5,4},{6,5},{7,6},{4,7},{9,8},{10,9},{11,1... | collective-permute-start | bytes 1179656 | tf_op jit(solution)/shard_map/ppermute | solution.py:17
  98.7 5.4 %collective-permute-start.14 = (f32[2,384,128]{2,1,0:T(8,128)S(1)}, f32[2,384,128]{2,1,0:T(8,128)S(1)}, u32[]{:S(2)}, u32[]{:S(2)}) collective-permute-start(f32[2,384,128]{2,1,0:T(8,128)S(1)} %slice.498), channel_id=1, source_target_pairs={{1,0},{2,1},{3,2},{0,3},{5,4},{6,5},{7,6},{4,7},{9,8},{10,9},{11,1... | collective-permute-start | bytes 1179656 | tf_op jit(solution)/shard_map/ppermute | solution.py:17
  112.0 7.6 %collective-permute-start.16 = (f32[2,384,128]{2,1,0:T(8,128)S(1)}, f32[2,384,128]{2,1,0:T(8,128)S(1)}, u32[]{:S(2)}, u32[]{:S(2)}) collective-permute-start(f32[2,384,128]{2,1,0:T(8,128)S(1)} %get-tuple-element.231), channel_id=1, source_target_pairs={{3,0},{0,1},{1,2},{2,3},{7,4},{4,5},{5,6},{6,7},{11,8},{8,9},{9,10... | collective-permute-start | bytes 1179656 | tf_op jit(solution)/shard_map/ppermute | solution.py:17
  116.9 7.9 %collective-permute-start.18 = (f32[2,384,128]{2,1,0:T(8,128)S(1)}, f32[2,384,128]{2,1,0:T(8,128)S(1)}, u32[]{:S(2)}, u32[]{:S(2)}) collective-permute-start(f32[2,384,128]{2,1,0:T(8,128)S(1)} %get-tuple-element.236), channel_id=1, source_target_pairs={{3,0},{0,1},{1,2},{2,3},{7,4},{4,5},{5,6},{6,7},{11,8},{8,9},{9,10... | collective-permute-start | bytes 1179656 | tf_op jit(solution)/shard_map/ppermute | solution.py:17
  119.8 10.0 %collective-permute-start.19 = (f32[2,128,256]{2,1,0:T(8,128)S(1)}, f32[2,128,256]{2,1,0:T(8,128)S(1)}, u32[]{:S(2)}, u32[]{:S(2)}) collective-permute-start(f32[2,128,256]{2,1,0:T(8,128)S(1)} %slice.500), channel_id=1, source_target_pairs={{28,0},{0,4},{4,8},{8,12},{12,16},{16,20},{20,24},{24,28},{29,1},{... | collective-permute-start | bytes 786440 | tf_op jit(solution)/shard_map/ppermute | solution.py:17
  124.8 7.3 %collective-permute-start.17 = (f32[2,384,128]{2,1,0:T(8,128)S(1)}, f32[2,384,128]{2,1,0:T(8,128)S(1)}, u32[]{:S(2)}, u32[]{:S(2)}) collective-permute-start(f32[2,384,128]{2,1,0:T(8,128)S(1)} %get-tuple-element.234), channel_id=1, source_target_pairs={{3,0},{0,1},{1,2},{2,3},{7,4},{4,5},{5,6},{6,7},{11,8},{8,9},{9,10... | collective-permute-start | bytes 1179656 | tf_op jit(solution)/shard_map/ppermute | solution.py:17
  129.9 9.1 %collective-permute-start.20 = (f32[2,128,256]{2,1,0:T(8,128)S(1)}, f32[2,128,256]{2,1,0:T(8,128)S(1)}, u32[]{:S(2)}, u32[]{:S(2)}) collective-permute-start(f32[2,128,256]{2,1,0:T(8,128)S(1)} %slice.471), channel_id=1, source_target_pairs={{28,0},{0,4},{4,8},{8,12},{12,16},{16,20},{20,24},{24,28},{29,1},{... | collective-permute-start | bytes 786440 | tf_op jit(solution)/shard_map/ppermute | solution.py:17
  139.0 9.1 %collective-permute-start.21 = (f32[2,128,256]{2,1,0:T(8,128)S(1)}, f32[2,128,256]{2,1,0:T(8,128)S(1)}, u32[]{:S(2)}, u32[]{:S(2)}) collective-permute-start(f32[2,128,256]{2,1,0:T(8,128)S(1)} %slice.474), channel_id=1, source_target_pairs={{28,0},{0,4},{4,8},{8,12},{12,16},{16,20},{20,24},{24,28},{29,1},{... | collective-permute-start | bytes 786440 | tf_op jit(solution)/shard_map/ppermute | solution.py:17
  (4 other events, 6.9 us)

commit v2 on v0

--- a/solution.py
+++ b/solution.py
@@ -9,6 +9,7 @@
 ITERS = 2
 STEP = 0.05
 SUB = 8
+GROUP = 6
 F32, BF16 = jnp.float32, jnp.bfloat16
 
 
@@ -29,9 +30,7 @@
 
     ah, al = halves(np.block([[c, s], [-s, c]]))
     bh, bl = halves(np.block([[c, -s], [s, c]]))
-    right = [np.concatenate([x, x, y], 0) for x, y in ((ah, al), (bh, bl))]
-    left = [np.concatenate([x, x, y], 1) for x, y in ((bh, bl), (ah, al))]
-    return np.stack(right), np.stack(left)
+    return np.stack([ah, bh]), np.stack([al, bl])
 
 
 def split(x):
@@ -112,7 +111,7 @@
 
 
 def groups(n):
-    size = 2 if n % 2 == 0 else 1
+    size = GROUP if n % GROUP == 0 else 1
     return [list(range(i, i + size)) for i in range(0, n, size)]
 
 
@@ -132,7 +131,8 @@
 
 
 def tab_of(tr, tl):
-    return ([tr[0], tr[1]], [tl[0], tl[1]])
+    pairs = [(tr[i], tl[i]) for i in range(2)]
+    return ([jnp.concatenate([x, x, y], 0) for x, y in pairs], [jnp.concatenate([x, x, y], 1) for x, y in pairs[::-1]])
 
 
 def rows_of(ps, h):

time: 143 us -> 135 us (0.944)
  Pallas kernels: 39.5 us -> 30.3 us
  starting transfers between devices: 28.2 us -> 32.2 us
  waiting for transfers between devices: 69.4 us -> 67 us
    pallas_call x10, Pallas kernels: 39.5 us -> 30.3 us  [call(): pl.pallas_call(body, out_shape=outs, in_specs=[pl.BlockSpec(memory_space=...]
    ppermute x24, starting transfers between devices: 28.2 us -> 32.2 us  [passed_along(): lax.ppermute(block, axis, [((i - distance) % n, i) for i in range(n)])]
    ppermute x24, waiting for transfers between devices: 69.4 us -> 67 us  [passed_along(): lax.ppermute(block, axis, [((i - distance) % n, i) for i in range(n)])]
  transfers between devices with their start and end apart: 24 -> 24, of which waited for: 15 -> 16; matrix products, arithmetic and copies ran while one was open for 2% -> 2% of each run, Pallas kernels for 16% -> 13%
where the time goes in v2:
time: 135 us
  waiting for transfers between devices  67 us (50%)
  starting transfers between devices  32.2 us (24%)
  Pallas kernels  30.3 us (22%)
  local copies, waits for them, and re-layouts  3.43 us (3%)
  other arithmetic  1.85 us (1%)
    ppermute x24, waiting for transfers between devices, passed_along(): lax.ppermute(block, axis, [((i - distance) % n, i) for i in range(n)])  67 us
    ppermute x24, starting transfers between devices, passed_along(): lax.ppermute(block, axis, [((i - distance) % n, i) for i in range(n)])  32.2 us
    pallas_call x10, Pallas kernels, call(): pl.pallas_call(body, out_shape=outs, in_specs=[pl.BlockSpec(memory_space=...  30.3 us
  transfers between devices with their start and end apart: 24, of which 16 were waited for; matrix products, arithmetic and copies ran while one was open for 2% of the time, Pallas kernels for 13%

profile of v2, /device:TPU:0, one launch (start us, length us, event | category | flops | bytes accessed | tf_op | source)
XLA Modules:
  0.0 135.3 jit_solution(5709722782576798393)
XLA Ops:
  1.5 6.1 %collective-permute-start.3 = (f32[2,128,256]{2,1,0:T(8,128)S(1)}, f32[2,128,256]{2,1,0:T(8,128)S(1)}, u32[]{:S(2)}, u32[]{:S(2)}) collective-permute-start(f32[2,128,256]{2,1,0:T(8,128)S(1)} %slice.481), channel_id=1, source_target_pairs={{4,0},{8,4},{12,8},{16,12},{20,16},{24,20},{28,24},{0,28},{5,1},{9... | collective-permute-start | bytes 786440 | tf_op jit(solution)/shard_map/ppermute | solution.py:18
  10.0 4.3 %collective-permute-done.3 = f32[2,128,256]{2,1,0:T(8,128)S(1)} collective-permute-done((f32[2,128,256]{2,1,0:T(8,128)S(1)}, f32[2,128,256]{2,1,0:T(8,128)S(1)}, u32[]{:S(2)}, u32[]{:S(2)}) %collective-permute-start.3) | collective-permute-done | bytes 262176 | tf_op jit(solution)/shard_map/ppermute | solution.py:18
  14.4 5.5 %collective-permute-done.1 = f32[2,128,256]{2,1,0:T(8,128)S(1)} collective-permute-done((f32[2,128,256]{2,1,0:T(8,128)S(1)}, f32[2,128,256]{2,1,0:T(8,128)S(1)}, u32[]{:S(2)}, u32[]{:S(2)}) %collective-permute-start.1) | collective-permute-done | bytes 262176 | tf_op jit(solution)/shard_map/ppermute | solution.py:18
  20.0 4.4 %collective-permute-done = f32[2,128,256]{2,1,0:T(8,128)S(1)} collective-permute-done((f32[2,128,256]{2,1,0:T(8,128)S(1)}, f32[2,128,256]{2,1,0:T(8,128)S(1)}, u32[]{:S(2)}, u32[]{:S(2)}) %collective-permute-start) | collective-permute-done | bytes 262176 | tf_op jit(solution)/shard_map/ppermute | solution.py:18
  24.7 5.1 %collective-permute-done.5.right = f32[2,384,128]{2,1,0:T(8,128)S(1)} collective-permute-done((f32[2,384,128]{2,1,0:T(8,128)S(1)}, f32[2,384,128]{2,1,0:T(8,128)S(1)}, u32[]{:S(2)}, u32[]{:S(2)}) %collective-permute-start.5) | collective-permute-done | bytes 393248 | tf_op jit(solution)/shard_map/ppermute | solution.py:18
  32.7 2.9 %shard_map.74 = (f32[768,256]{1,0:T(8,128)S(1)}, f32[768,256]{1,0:T(8,128)S(1)}) custom-call(s32[6,2]{1,0:T(8,128)S(1)} %copy.15.offs, f32[2,384,256]{2,1,0:T(8,128)S(1)} %pad_maximum_fusion.3.tall, f32[2,384,128]{2,1,0:T(8,128)S(1)} %collective-permute-done.4.right, f32[768,256]{1,0:T(8,128)S(1)} %shard_map.73.w_in, ...), custom_call_target="tpu_custom_call" | custom-call | flops 1207959552 | bytes 6000000 | tf_op jit(solution)/shard_map/pallas_call | solution.py:228
  35.6 3.3 %shard_map.75 = (f32[2,384,256]{2,1,0:T(8,128)S(1)}, f32[2,384,128]{2,1,0:T(8,128)S(1)}, f32[768,256]{1,0:T(8,128)S(1)}) custom-call(s32[6,2]{1,0:T(8,128)S(1)} %copy.15.offs, f32[2,384,256]{2,1,0:T(8,128)S(1)} %pad_maximum_fusion.2.tall, f32[2,384,128]{2,1,0:T(8,128)S(1)} %collective-permute-done.2.right, f32[768,256]{1,0:T(8,128)S(1)} %get-tuple-element.205.w_in, ...), custom_call_target="tpu_custom_call" | custom-call | flops 1207959552 | bytes 6000000 | tf_op jit(solution)/shard_map/pallas_call | solution.py:228
  38.9 3.1 %shard_map.76 = (f32[2,384,256]{2,1,0:T(8,128)S(1)}, f32[2,384,128]{2,1,0:T(8,128)S(1)}, f32[768,256]{1,0:T(8,128)S(1)}) custom-call(s32[6,2]{1,0:T(8,128)S(1)} %copy.15.offs, f32[768,256]{1,0:T(8,128)S(1)} %get-tuple-element.206.g_in, f32[768,256]{1,0:T(8,128)S(1)} %shard_map.73.w_in, f32[768,256]{1,0:T(8,128)S(1)} %get-tuple-element.207.o_in, ...), custom_call_target="tpu_custom_call" | custom-call | flops 1207959552 | bytes 6000000 | tf_op jit(solution)/shard_map/pallas_call | solution.py:228
  42.0 3.0 %shard_map.77 = (f32[2,384,256]{2,1,0:T(8,128)S(1)}, f32[2,384,128]{2,1,0:T(8,128)S(1)}) custom-call(s32[6,2]{1,0:T(8,128)S(1)} %copy.15.offs, f32[768,256]{1,0:T(8,128)S(1)} %get-tuple-element.208.g_in, f32[2,128,128]{2,1,0:T(8,128)S(1)} %copy-done.1, f32[2,128,128]{2,1,0:T(8,128)S(1)} %pad_maximum_fusion.4.phase, bf16[2,256,256]{2,1,0:T(8,128)(2,1)S(1)} %copy-done.3, ...), custom_call_target="tpu_custom_call" | custom-call | flops 1207959552 | bytes 6000000 | tf_op jit(solution)/shard_map/pallas_call | solution.py:228
  47.5 4.9 %collective-permute-done.6 = f32[2,384,128]{2,1,0:T(8,128)S(1)} collective-permute-done((f32[2,384,128]{2,1,0:T(8,128)S(1)}, f32[2,384,128]{2,1,0:T(8,128)S(1)}, u32[]{:S(2)}, u32[]{:S(2)}) %collective-permute-start.6) | collective-permute-done | bytes 393248 | tf_op jit(solution)/shard_map/ppermute | solution.py:18
  52.9 3.7 %collective-permute-done.13 = f32[2,384,128]{2,1,0:T(8,128)S(1)} collective-permute-done((f32[2,384,128]{2,1,0:T(8,128)S(1)}, f32[2,384,128]{2,1,0:T(8,128)S(1)}, u32[]{:S(2)}, u32[]{:S(2)}) %collective-permute-start.13) | collective-permute-done | bytes 393248 | tf_op jit(solution)/shard_map/ppermute | solution.py:18
  57.2 3.7 %collective-permute-done.9 = f32[2,384,128]{2,1,0:T(8,128)S(1)} collective-permute-done((f32[2,384,128]{2,1,0:T(8,128)S(1)}, f32[2,384,128]{2,1,0:T(8,128)S(1)}, u32[]{:S(2)}, u32[]{:S(2)}) %collective-permute-start.9) | collective-permute-done | bytes 393248 | tf_op jit(solution)/shard_map/ppermute | solution.py:18
  61.4 3.3 %collective-permute-done.7 = f32[2,128,256]{2,1,0:T(8,128)S(1)} collective-permute-done((f32[2,128,256]{2,1,0:T(8,128)S(1)}, f32[2,128,256]{2,1,0:T(8,128)S(1)}, u32[]{:S(2)}, u32[]{:S(2)}) %collective-permute-start.7) | collective-permute-done | bytes 262176 | tf_op jit(solution)/shard_map/ppermute | solution.py:18
  66.5 3.8 %collective-permute-done.14 = f32[2,128,256]{2,1,0:T(8,128)S(1)} collective-permute-done((f32[2,128,256]{2,1,0:T(8,128)S(1)}, f32[2,128,256]{2,1,0:T(8,128)S(1)}, u32[]{:S(2)}, u32[]{:S(2)}) %collective-permute-start.14) | collective-permute-done | bytes 262176 | tf_op jit(solution)/shard_map/ppermute | solution.py:18
  70.5 10.1 %collective-permute-start.15 = (f32[2,128,256]{2,1,0:T(8,128)S(1)}, f32[2,128,256]{2,1,0:T(8,128)S(1)}, u32[]{:S(2)}, u32[]{:S(2)}) collective-permute-start(f32[2,128,256]{2,1,0:T(8,128)S(1)} %get-tuple-element.230), channel_id=1, source_target_pairs={{4,0},{8,4},{12,8},{16,12},{20,16},{24,20},{28,24},{0,28},{5,1},{9... | collective-permute-start | bytes 786440 | tf_op jit(solution)/shard_map/ppermute | solution.py:18
  80.7 4.2 %collective-permute-start.11 = (f32[2,128,256]{2,1,0:T(8,128)S(1)}, f32[2,128,256]{2,1,0:T(8,128)S(1)}, u32[]{:S(2)}, u32[]{:S(2)}) collective-permute-start(f32[2,128,256]{2,1,0:T(8,128)S(1)} %get-tuple-element.232), channel_id=1, source_target_pairs={{4,0},{8,4},{12,8},{16,12},{20,16},{24,20},{28,24},{0,28},{5,1},{9... | collective-permute-start | bytes 786440 | tf_op jit(solution)/shard_map/ppermute | solution.py:18
  86.3 5.2 %collective-permute-done.11 = f32[2,128,256]{2,1,0:T(8,128)S(1)} collective-permute-done((f32[2,128,256]{2,1,0:T(8,128)S(1)}, f32[2,128,256]{2,1,0:T(8,128)S(1)}, u32[]{:S(2)}, u32[]{:S(2)}) %collective-permute-start.11) | collective-permute-done | bytes 262176 | tf_op jit(solution)/shard_map/ppermute | solution.py:18
  94.8 2.9 %shard_map.79 = (f32[768,256]{1,0:T(8,128)S(1)}, f32[768,256]{1,0:T(8,128)S(1)}) custom-call(s32[6,2]{1,0:T(8,128)S(1)} %copy.15.offs, f32[2,384,256]{2,1,0:T(8,128)S(1)} %multiply_subtract_fusion.tall, f32[2,384,128]{2,1,0:T(8,128)S(1)} %collective-permute-done.16.right, f32[768,256]{1,0:T(8,128)S(1)} %shard_map.78.w_in, ...), custom_call_target="tpu_custom_call" | custom-call | flops 1207959552 | bytes 6000000 | tf_op jit(solution)/shard_map/pallas_call | solution.py:228
  98.9 3.3 %shard_map.80 = (f32[2,384,256]{2,1,0:T(8,128)S(1)}, f32[2,384,128]{2,1,0:T(8,128)S(1)}, f32[768,256]{1,0:T(8,128)S(1)}) custom-call(s32[6,2]{1,0:T(8,128)S(1)} %copy.15.offs, f32[2,384,256]{2,1,0:T(8,128)S(1)} %multiply_subtract_fusion.1.tall, f32[2,384,128]{2,1,0:T(8,128)S(1)} %collective-permute-done.12.right, f32[768,256]{1,0:T(8,128)S(1)} %get-tuple-element.215.w_in, ...), custom_call_target="tpu_custom_call" | custom-call | flops 1207959552 | bytes 6000000 | tf_op jit(solution)/shard_map/pallas_call | solution.py:228
  103.0 3.1 %shard_map.81 = (f32[2,384,256]{2,1,0:T(8,128)S(1)}, f32[2,384,128]{2,1,0:T(8,128)S(1)}, f32[768,256]{1,0:T(8,128)S(1)}) custom-call(s32[6,2]{1,0:T(8,128)S(1)} %copy.15.offs, f32[768,256]{1,0:T(8,128)S(1)} %get-tuple-element.216.g_in, f32[768,256]{1,0:T(8,128)S(1)} %shard_map.78.w_in, f32[768,256]{1,0:T(8,128)S(1)} %get-tuple-element.217.o_in, ...), custom_call_target="tpu_custom_call" | custom-call | flops 1207959552 | bytes 6000000 | tf_op jit(solution)/shard_map/pallas_call | solution.py:228
  106.5 3.0 %shard_map.82 = (f32[2,384,256]{2,1,0:T(8,128)S(1)}, f32[2,384,128]{2,1,0:T(8,128)S(1)}) custom-call(s32[6,2]{1,0:T(8,128)S(1)} %copy.15.offs, f32[768,256]{1,0:T(8,128)S(1)} %get-tuple-element.218.g_in, f32[2,128,128]{2,1,0:T(8,128)S(1)} %copy-done.1, f32[2,128,128]{2,1,0:T(8,128)S(1)} %pad_maximum_fusion.4.phase, bf16[2,256,256]{2,1,0:T(8,128)(2,1)S(1)} %copy-done.3, ...), custom_call_target="tpu_custom_call" | custom-call | flops 1207959552 | bytes 6000000 | tf_op jit(solution)/shard_map/pallas_call | solution.py:228
  114.0 4.0 %collective-permute-done.18 = f32[2,384,128]{2,1,0:T(8,128)S(1)} collective-permute-done((f32[2,384,128]{2,1,0:T(8,128)S(1)}, f32[2,384,128]{2,1,0:T(8,128)S(1)}, u32[]{:S(2)}, u32[]{:S(2)}) %collective-permute-start.18) | collective-permute-done | bytes 393248 | tf_op jit(solution)/shard_map/ppermute | solution.py:18
  119.1 3.1 %collective-permute-done.23 = f32[2,128,256]{2,1,0:T(8,128)S(1)} collective-permute-done((f32[2,128,256]{2,1,0:T(8,128)S(1)}, f32[2,128,256]{2,1,0:T(8,128)S(1)}, u32[]{:S(2)}, u32[]{:S(2)}) %collective-permute-start.23) | collective-permute-done | bytes 262176 | tf_op jit(solution)/shard_map/ppermute | solution.py:18
  122.3 11.4 %collective-permute-done.21 = f32[2,128,256]{2,1,0:T(8,128)S(1)} collective-permute-done((f32[2,128,256]{2,1,0:T(8,128)S(1)}, f32[2,128,256]{2,1,0:T(8,128)S(1)}, u32[]{:S(2)}, u32[]{:S(2)}) %collective-permute-start.21) | collective-permute-done | bytes 262176 | tf_op jit(solution)/shard_map/ppermute | solution.py:18
  (94 shorter events, 27.4 us)
Async XLA Ops:
  1.5 12.8 %collective-permute-start.3 = (f32[2,128,256]{2,1,0:T(8,128)S(1)}, f32[2,128,256]{2,1,0:T(8,128)S(1)}, u32[]{:S(2)}, u32[]{:S(2)}) collective-permute-start(f32[2,128,256]{2,1,0:T(8,128)S(1)} %slice.481), channel_id=1, source_target_pairs={{4,0},{8,4},{12,8},{16,12},{20,16},{24,20},{28,24},{0,28},{5,1},{9... | collective-permute-start | bytes 786440 | tf_op jit(solution)/shard_map/ppermute | solution.py:18
  7.6 12.3 %collective-permute-start.1 = (f32[2,128,256]{2,1,0:T(8,128)S(1)}, f32[2,128,256]{2,1,0:T(8,128)S(1)}, u32[]{:S(2)}, u32[]{:S(2)}) collective-permute-start(f32[2,128,256]{2,1,0:T(8,128)S(1)} %slice.478), channel_id=1, source_target_pairs={{4,0},{8,4},{12,8},{16,12},{20,16},{24,20},{28,24},{0,28},{5,1},{9... | collective-permute-start | bytes 786440 | tf_op jit(solution)/shard_map/ppermute | solution.py:18
  8.2 16.2 %collective-permute-start = (f32[2,128,256]{2,1,0:T(8,128)S(1)}, f32[2,128,256]{2,1,0:T(8,128)S(1)}, u32[]{:S(2)}, u32[]{:S(2)}) collective-permute-start(f32[2,128,256]{2,1,0:T(8,128)S(1)} %slice.477), channel_id=1, source_target_pairs={{4,0},{8,4},{12,8},{16,12},{20,16},{24,20},{28,24},{0,28},{5,1},{9... | collective-permute-start | bytes 786440 | tf_op jit(solution)/shard_map/ppermute | solution.py:18
  14.3 18.4 %collective-permute-start.4 = (f32[2,384,128]{2,1,0:T(8,128)S(1)}, f32[2,384,128]{2,1,0:T(8,128)S(1)}, u32[]{:S(2)}, u32[]{:S(2)}) collective-permute-start(f32[2,384,128]{2,1,0:T(8,128)S(1)} %fusion.3), channel_id=1, source_target_pairs={{1,0},{2,1},{3,2},{0,3},{5,4},{6,5},{7,6},{4,7},{9,8},{10,9},{11,1... | collective-permute-start | bytes 1179656 | tf_op jit(solution)/shard_map/ppermute | solution.py:18
  19.9 15.7 %collective-permute-start.2 = (f32[2,384,128]{2,1,0:T(8,128)S(1)}, f32[2,384,128]{2,1,0:T(8,128)S(1)}, u32[]{:S(2)}, u32[]{:S(2)}) collective-permute-start(f32[2,384,128]{2,1,0:T(8,128)S(1)} %fusion.4), channel_id=1, source_target_pairs={{1,0},{2,1},{3,2},{0,3},{5,4},{6,5},{7,6},{4,7},{9,8},{10,9},{11,1... | collective-permute-start | bytes 1179656 | tf_op jit(solution)/shard_map/ppermute | solution.py:18
  24.4 5.4 %collective-permute-start.5 = (f32[2,384,128]{2,1,0:T(8,128)S(1)}, f32[2,384,128]{2,1,0:T(8,128)S(1)}, u32[]{:S(2)}, u32[]{:S(2)}) collective-permute-start(f32[2,384,128]{2,1,0:T(8,128)S(1)} %fusion.5), channel_id=1, source_target_pairs={{1,0},{2,1},{3,2},{0,3},{5,4},{6,5},{7,6},{4,7},{9,8},{10,9},{11,1... | collective-permute-start | bytes 1179656 | tf_op jit(solution)/shard_map/ppermute | solution.py:18
  45.0 7.4 %collective-permute-start.6 = (f32[2,384,128]{2,1,0:T(8,128)S(1)}, f32[2,384,128]{2,1,0:T(8,128)S(1)}, u32[]{:S(2)}, u32[]{:S(2)}) collective-permute-start(f32[2,384,128]{2,1,0:T(8,128)S(1)} %get-tuple-element.210), channel_id=1, source_target_pairs={{3,0},{0,1},{1,2},{2,3},{7,4},{4,5},{5,6},{6,7},{11,8},{8,9},{9,10... | collective-permute-start | bytes 1179656 | tf_op jit(solution)/shard_map/ppermute | solution.py:18
  46.8 9.9 %collective-permute-start.13 = (f32[2,384,128]{2,1,0:T(8,128)S(1)}, f32[2,384,128]{2,1,0:T(8,128)S(1)}, u32[]{:S(2)}, u32[]{:S(2)}) collective-permute-start(f32[2,384,128]{2,1,0:T(8,128)S(1)} %get-tuple-element.214), channel_id=1, source_target_pairs={{3,0},{0,1},{1,2},{2,3},{7,4},{4,5},{5,6},{6,7},{11,8},{8,9},{9,10... | collective-permute-start | bytes 1179656 | tf_op jit(solution)/shard_map/ppermute | solution.py:18
  46.9 14.0 %collective-permute-start.9 = (f32[2,384,128]{2,1,0:T(8,128)S(1)}, f32[2,384,128]{2,1,0:T(8,128)S(1)}, u32[]{:S(2)}, u32[]{:S(2)}) collective-permute-start(f32[2,384,128]{2,1,0:T(8,128)S(1)} %get-tuple-element.212), channel_id=1, source_target_pairs={{3,0},{0,1},{1,2},{2,3},{7,4},{4,5},{5,6},{6,7},{11,8},{8,9},{9,10... | collective-permute-start | bytes 1179656 | tf_op jit(solution)/shard_map/ppermute | solution.py:18
  52.6 12.1 %collective-permute-start.7 = (f32[2,128,256]{2,1,0:T(8,128)S(1)}, f32[2,128,256]{2,1,0:T(8,128)S(1)}, u32[]{:S(2)}, u32[]{:S(2)}) collective-permute-start(f32[2,128,256]{2,1,0:T(8,128)S(1)} %slice.487), channel_id=1, source_target_pairs={{28,0},{0,4},{4,8},{8,12},{12,16},{16,20},{20,24},{24,28},{29,1},{... | collective-permute-start | bytes 786440 | tf_op jit(solution)/shard_map/ppermute | solution.py:18
  56.8 13.6 %collective-permute-start.14 = (f32[2,128,256]{2,1,0:T(8,128)S(1)}, f32[2,128,256]{2,1,0:T(8,128)S(1)}, u32[]{:S(2)}, u32[]{:S(2)}) collective-permute-start(f32[2,128,256]{2,1,0:T(8,128)S(1)} %slice.495), channel_id=1, source_target_pairs={{28,0},{0,4},{4,8},{8,12},{12,16},{16,20},{20,24},{24,28},{29,1},{... | collective-permute-start | bytes 786440 | tf_op jit(solution)/shard_map/ppermute | solution.py:18
  61.0 19.6 %collective-permute-start.10 = (f32[2,128,256]{2,1,0:T(8,128)S(1)}, f32[2,128,256]{2,1,0:T(8,128)S(1)}, u32[]{:S(2)}, u32[]{:S(2)}) collective-permute-start(f32[2,128,256]{2,1,0:T(8,128)S(1)} %slice.491), channel_id=1, source_target_pairs={{28,0},{0,4},{4,8},{8,12},{12,16},{16,20},{20,24},{24,28},{29,1},{... | collective-permute-start | bytes 786440 | tf_op jit(solution)/shard_map/ppermute | solution.py:18
  64.8 20.1 %collective-permute-start.8 = (f32[2,128,256]{2,1,0:T(8,128)S(1)}, f32[2,128,256]{2,1,0:T(8,128)S(1)}, u32[]{:S(2)}, u32[]{:S(2)}) collective-permute-start(f32[2,128,256]{2,1,0:T(8,128)S(1)} %get-tuple-element.228), channel_id=1, source_target_pairs={{4,0},{8,4},{12,8},{16,12},{20,16},{24,20},{28,24},{0,28},{5,1},{9... | collective-permute-start | bytes 786440 | tf_op jit(solution)/shard_map/ppermute | solution.py:18
  70.5 15.4 %collective-permute-start.15 = (f32[2,128,256]{2,1,0:T(8,128)S(1)}, f32[2,128,256]{2,1,0:T(8,128)S(1)}, u32[]{:S(2)}, u32[]{:S(2)}) collective-permute-start(f32[2,128,256]{2,1,0:T(8,128)S(1)} %get-tuple-element.230), channel_id=1, source_target_pairs={{4,0},{8,4},{12,8},{16,12},{20,16},{24,20},{28,24},{0,28},{5,1},{9... | collective-permute-start | bytes 786440 | tf_op jit(solution)/shard_map/ppermute | solution.py:18
  80.7 10.8 %collective-permute-start.11 = (f32[2,128,256]{2,1,0:T(8,128)S(1)}, f32[2,128,256]{2,1,0:T(8,128)S(1)}, u32[]{:S(2)}, u32[]{:S(2)}) collective-permute-start(f32[2,128,256]{2,1,0:T(8,128)S(1)} %get-tuple-element.232), channel_id=1, source_target_pairs={{4,0},{8,4},{12,8},{16,12},{20,16},{24,20},{28,24},{0,28},{5,1},{9... | collective-permute-start | bytes 786440 | tf_op jit(solution)/shard_map/ppermute | solution.py:18
  85.1 6.8 %collective-permute-start.17 = (f32[2,384,128]{2,1,0:T(8,128)S(1)}, f32[2,384,128]{2,1,0:T(8,128)S(1)}, u32[]{:S(2)}, u32[]{:S(2)}) collective-permute-start(f32[2,384,128]{2,1,0:T(8,128)S(1)} %slice.498), channel_id=1, source_target_pairs={{1,0},{2,1},{3,2},{0,3},{5,4},{6,5},{7,6},{4,7},{9,8},{10,9},{11,1... | collective-permute-start | bytes 1179656 | tf_op jit(solution)/shard_map/ppermute | solution.py:18
  86.1 8.6 %collective-permute-start.16 = (f32[2,384,128]{2,1,0:T(8,128)S(1)}, f32[2,384,128]{2,1,0:T(8,128)S(1)}, u32[]{:S(2)}, u32[]{:S(2)}) collective-permute-start(f32[2,384,128]{2,1,0:T(8,128)S(1)} %slice.497), channel_id=1, source_target_pairs={{1,0},{2,1},{3,2},{0,3},{5,4},{6,5},{7,6},{4,7},{9,8},{10,9},{11,1... | collective-permute-start | bytes 1179656 | tf_op jit(solution)/shard_map/ppermute | solution.py:18
  91.6 7.2 %collective-permute-start.12 = (f32[2,384,128]{2,1,0:T(8,128)S(1)}, f32[2,384,128]{2,1,0:T(8,128)S(1)}, u32[]{:S(2)}, u32[]{:S(2)}) collective-permute-start(f32[2,384,128]{2,1,0:T(8,128)S(1)} %slice.493), channel_id=1, source_target_pairs={{1,0},{2,1},{3,2},{0,3},{5,4},{6,5},{7,6},{4,7},{9,8},{10,9},{11,1... | collective-permute-start | bytes 1179656 | tf_op jit(solution)/shard_map/ppermute | solution.py:18
  102.2 8.9 %collective-permute-start.22 = (f32[2,384,128]{2,1,0:T(8,128)S(1)}, f32[2,384,128]{2,1,0:T(8,128)S(1)}, u32[]{:S(2)}, u32[]{:S(2)}) collective-permute-start(f32[2,384,128]{2,1,0:T(8,128)S(1)} %get-tuple-element.224), channel_id=1, source_target_pairs={{3,0},{0,1},{1,2},{2,3},{7,4},{4,5},{5,6},{6,7},{11,8},{8,9},{9,10... | collective-permute-start | bytes 1179656 | tf_op jit(solution)/shard_map/ppermute | solution.py:18
  106.2 7.6 %collective-permute-start.20 = (f32[2,384,128]{2,1,0:T(8,128)S(1)}, f32[2,384,128]{2,1,0:T(8,128)S(1)}, u32[]{:S(2)}, u32[]{:S(2)}) collective-permute-start(f32[2,384,128]{2,1,0:T(8,128)S(1)} %get-tuple-element.222), channel_id=1, source_target_pairs={{3,0},{0,1},{1,2},{2,3},{7,4},{4,5},{5,6},{6,7},{11,8},{8,9},{9,10... | collective-permute-start | bytes 1179656 | tf_op jit(solution)/shard_map/ppermute | solution.py:18
  109.5 8.5 %collective-permute-start.18 = (f32[2,384,128]{2,1,0:T(8,128)S(1)}, f32[2,384,128]{2,1,0:T(8,128)S(1)}, u32[]{:S(2)}, u32[]{:S(2)}) collective-permute-start(f32[2,384,128]{2,1,0:T(8,128)S(1)} %get-tuple-element.220), channel_id=1, source_target_pairs={{3,0},{0,1},{1,2},{2,3},{7,4},{4,5},{5,6},{6,7},{11,8},{8,9},{9,10... | collective-permute-start | bytes 1179656 | tf_op jit(solution)/shard_map/ppermute | solution.py:18
  111.2 11.0 %collective-permute-start.23 = (f32[2,128,256]{2,1,0:T(8,128)S(1)}, f32[2,128,256]{2,1,0:T(8,128)S(1)}, u32[]{:S(2)}, u32[]{:S(2)}) collective-permute-start(f32[2,128,256]{2,1,0:T(8,128)S(1)} %slice.509), channel_id=1, source_target_pairs={{28,0},{0,4},{4,8},{8,12},{12,16},{16,20},{20,24},{24,28},{29,1},{... | collective-permute-start | bytes 786440 | tf_op jit(solution)/shard_map/ppermute | solution.py:18
  118.2 15.7 %collective-permute-start.19 = (f32[2,128,256]{2,1,0:T(8,128)S(1)}, f32[2,128,256]{2,1,0:T(8,128)S(1)}, u32[]{:S(2)}, u32[]{:S(2)}) collective-permute-start(f32[2,128,256]{2,1,0:T(8,128)S(1)} %slice.501), channel_id=1, source_target_pairs={{28,0},{0,4},{4,8},{8,12},{12,16},{16,20},{20,24},{24,28},{29,1},{... | collective-permute-start | bytes 786440 | tf_op jit(solution)/shard_map/ppermute | solution.py:18
  118.2 15.5 %collective-permute-start.21 = (f32[2,128,256]{2,1,0:T(8,128)S(1)}, f32[2,128,256]{2,1,0:T(8,128)S(1)}, u32[]{:S(2)}, u32[]{:S(2)}) collective-permute-start(f32[2,128,256]{2,1,0:T(8,128)S(1)} %slice.505), channel_id=1, source_target_pairs={{28,0},{0,4},{4,8},{8,12},{12,16},{16,20},{20,24},{24,28},{29,1},{... | collective-permute-start | bytes 786440 | tf_op jit(solution)/shard_map/ppermute | solution.py:18
  (6 other events, 35.2 us)
